TPU v7x, 32 devices: a whole 2x2x4 slice. The times are simulated.
32 devices in a mesh: dom: 32 (over z, y, x, core).
Axes of the slice: x: 2, y: 2, z: 4, core: 2. Of those that a mesh axis runs over, the one named last changes fastest.
Arguments:
- adjoint_end: bfloat16 [256, 384, 256], P('dom'), may hold values from -6 to 6
- operator_blocks: bfloat16 [256, 6, 384, 384], P('dom'), may hold values from -0.125 to 0.125
- block_cols: int32 [256, 6], P('dom'), may hold values from -1 to 15, as said below
- halo_send: int32 [32, 4, 2], P('dom'), may hold values from -1 to 7, as said below
- wet_cells: int32 [256, 128], P('dom'), may hold values 0 or 1
- gauge_cells: int32 [256], replicated, may hold values from 0 to 32767
- window_first: int32 [256], replicated, may hold values from 0 to 1
- window_len: int32 [256], replicated, may hold values from 1 to 2
- gauge_gain: float32 [256], replicated, may hold values from 0.5 to 4
- snapshots: float32 [2, 256, 384], P(None, 'dom'), may hold values from -27 to 27, as said below
Outputs:
- adjoint_start: bfloat16 [256, 384, 256], P('dom')
- sensitivity: float32 [256, 128, 256], P('dom')
Inputs may be any that keep to these rules, and one draw needn't show every extreme that they name: `block_cols`: in each row entry 0 is the row's own local block; live entries come first and -1 fills the rest; received slots named are only those whose sending device exists. `halo_send`: for each device and neighbour o the 2 blocks are distinct; -1 exactly where device d + off_o does not exist. `snapshots`: nonzero values.
All inputs are finite; a program needn't handle non-finite values. No bound on the sum of `wet_cells` on one device may be relied on, other than what follows from the above.
Results may differ from a plain program's by a relative error of at most 0.0013.
The roundings to bfloat16 on the way count: a program that leaves them out, or rounds other values in their place, can miss the bound.
Values may be sent and summed in bfloat16 or wider, within the bound.
No kernel may reach another device: no remote copies, remote signals or barrier semaphores. Data moves between devices by JAX's collectives and lax.ppermute only.
A program may use at most 128 MiB of HBM per device.

v0:
```python
import functools

import jax
import jax.numpy as jnp
from jax import lax
from jax.experimental import pallas as pl
from jax.experimental.pallas import tpu as pltpu
from jax.sharding import PartitionSpec as P

PARTS = 2
PICK_COST = 4 << 20
EARLY_COST = 4 << 20
LATE_COST = ((4 << 20, 4 << 20), (4 << 20, 4 << 20))
SPLIT = ("inner", "outer", "cross")
FIRST = ("swap",) + SPLIT
ROUTES = ("swap",) + SPLIT


def route_pairs(devices):
    swap = [(i, i ^ 1) for i in range(devices)]
    cross = [(i, i + 1) for i in range(1, devices - 1, 2)]
    inner = [(i, i ^ 2) for i in range(devices)]
    outer = [(i, i + 2) for i in range(devices - 2) if i & 2]
    both = lambda pairs: pairs + [(j, i) for i, j in pairs]
    return dict(swap=swap, cross=both(cross), inner=inner, outer=both(outer))


def send_groups(device):
    core, chip = device % 2, (device // 2) % 2
    return dict(swap=2 - core, cross=1 + core, inner=3 - 3 * chip, outer=3 * chip)


def receive_groups(device):
    core, chip = device % 2, (device // 2) % 2
    return dict(swap=1 + core, cross=2 - core, inner=3 * chip, outer=3 - 3 * chip)


def exchange(sends):
    pairs = route_pairs(lax.axis_size("dom"))
    return {r: lax.ppermute(sent, "dom", pairs[r]) for r, sent in sends.items()}


def pinned(value):
    return pltpu.with_memory_space_constraint(value, pltpu.VMEM)


def in_hbm(value):
    return pltpu.with_memory_space_constraint(value, pltpu.HBM)


def pick_kernel(part, halo, lam, *rest):
    outs, sems = dict(zip(FIRST, rest[:4])), rest[4]
    groups = send_groups(lax.axis_index("dom"))
    copies = []
    for i, r in enumerate(FIRST):
        band = pl.ds(*(part if r in SPLIT else (0, lam.shape[2])))
        for c in range(2):
            row = jnp.maximum(halo[0, c, groups[r]], 0)
            copies.append(
                pltpu.make_async_copy(lam.at[row, :, band], outs[r].at[c], sems.at[i, c])
            )
    for copy in copies:
        copy.start()
    for copy in copies:
        copy.wait()


def pick_sends(part, cost, place, halo, lam):
    outs = pl.pallas_call(
        functools.partial(pick_kernel, part),
        name="pick_sends",
        out_shape=[
            pltpu.VMEM((2, lam.shape[1], part[1] if r in SPLIT else lam.shape[2]), lam.dtype)
            for r in FIRST
        ],
        in_specs=[pl.BlockSpec(memory_space=pltpu.SMEM), pl.BlockSpec(memory_space=place)],
        out_specs=[pl.BlockSpec(memory_space=pltpu.VMEM)] * 4,
        scratch_shapes=[pltpu.SemaphoreType.DMA((4, 2))],
        compiler_params=pltpu.CompilerParams(vmem_limit_bytes=4 * 1024 * 1024),
        cost_estimate=pl.CostEstimate(flops=0, bytes_accessed=cost, transcendentals=0),
    )(in_hbm(halo), pltpu.with_memory_space_constraint(lam, place))
    return dict(zip(FIRST, outs))


def lay_out_facts(facts, aux, gauges):
    wet, snapshots = facts[:2]
    owned, cells = wet.shape
    for i, fact in enumerate(facts[2:]):
        gauges[i : i + 1, :] = fact[...].astype(jnp.float32)
    for b in range(owned):
        rows = [wet[b : b + 1, :].astype(jnp.float32)]
        for t in range(snapshots.shape[0]):
            for c in range(3):
                rows.append(snapshots[t, b : b + 1, c * cells : (c + 1) * cells])
        rows.append(jnp.zeros((1, cells), jnp.float32))
        aux[b] = jnp.concatenate(rows, axis=0).T


def step_kernel(late, last, step, part, final, *refs):
    refs = list(refs)
    take = lambda n: [refs.pop(0) for _ in range(n)]
    cols, halo, lam, ops = take(4)
    begin = not late and step == 0
    facts = take(6) if begin else None
    aux, gauges = (None, None) if begin else take(2)
    received = dict(zip(ROUTES, take(4))) if late else {}
    take(1 + last if late else 0)
    done_squares = take(1)[0] if late and last else None
    base = take(1)[0] if late and last else None
    (new,) = take(1)
    raw, squares = take(2) if last else (None, None)
    base = take(1)[0] if last and not late else base
    sends = dict(zip(ROUTES, take(4))) if late and not last else {}
    if begin:
        aux, gauges, kept, kept_cols, kept_halo = take(5)
        ahead = [dict(zip(SPLIT, take(3))) for _ in range(PARTS - 1)]
        far, ops = ops, kept
    order = refs.pop(0)
    summed = refs.pop(0) if last else None
    (slots,) = refs if late else (None,)
    (op_sem,) = refs if begin else (None,)

    owned, entries = ops.shape[0], ops.shape[1]
    rows, width = lam.shape[1], part[1]
    cells = rows // 3
    here = pl.ds(*part)
    position = lax.axis_index("dom")

    def sent_rows(routes):
        groups = send_groups(position)
        return [(r, c, jnp.maximum(halo[0, c, groups[r]], 0)) for r in routes for c in range(2)]

    if late:
        groups = receive_groups(position)
        for r in ROUTES:
            slots[pl.ds(2 * groups[r], 2)] = (
                received[r][:, :, here] if r == "swap" and step == 0 else received[r][...]
            )
    if last:
        summed[...] = jnp.zeros(summed.shape, jnp.float32)

    def fetch(b, p):
        pair = pl.ds(2 * p, 2)
        return pltpu.make_async_copy(far.at[b, pair], ops.at[b, pair], op_sem.at[b, p])

    def for_pairs(b, act):
        number = shape_of(b)[0]
        for p in range(entries // 2):

            @pl.when(number > p)
            def _(p=p):
                act(fetch(b, p))

    def shape_of(b):
        live, top = 0, -1
        for k in range(entries):
            live = live + (cols[b, k] >= 0).astype(jnp.int32)
            top = jnp.maximum(top, cols[b, k])
        return (live + 1) // 2, (top >= owned) if late else (top < owned)

    if begin:

        for own in (True, False):

            @pl.loop(0, owned)
            def _(b, own=own):
                @pl.when(shape_of(b)[1] == own)
                def _():
                    for_pairs(b, lambda copy: copy.start())

        lay_out_facts(facts, aux, gauges)
        for b in range(owned):
            for k in range(entries):
                kept_cols[b, k] = cols[b, k]
        for c in range(halo.shape[1]):
            for o in range(halo.shape[2]):
                kept_halo[0, c, o] = halo[0, c, o]
        for i, picks in enumerate(ahead):
            band = pl.ds((i + 1) * (part[1] // PARTS), part[1] // PARTS)
            for r, c, row in sent_rows(SPLIT):
                picks[r][c] = lam[row, :, band]

    first = gauges[1:2, here]
    active = jnp.where(
        jnp.logical_and(first <= step, step < first + gauges[2:3, here]), gauges[3:4, here], 0.0
    )
    own_cells = lax.broadcasted_iota(jnp.int32, (cells, width), 0)

    def prepare(b, total):
        base[b] = lam[b, :, here].astype(jnp.float32) + total
        raw[b, :, here] = from_snapshot(0, b, lambda c: lam[b, pl.ds(c * cells, cells), here])

    def from_snapshot(t, b, state, gathered=None):
        for c in range(3):
            column = 1 + 3 * t + c
            term = aux[b, :, column : column + 1] * state(c).astype(jnp.float32)
            gathered = term if gathered is None else gathered + term
        return gathered

    def finish(b, total, counted=None):
        wet = aux[b, :, 0:1]
        where = gauges[0:1, here].astype(jnp.int32) - (position * owned + b) * cells
        source = jnp.where(own_cells == where, active, 0.0)
        made = []
        for c in range(3):
            band = pl.ds(c * cells, cells)
            if base is not None and late:
                before = base[b, band, here]
            else:
                before = lam[b, band, here].astype(jnp.float32)
            updated = wet * (before + total[c * cells : (c + 1) * cells])
            if c == 0:
                updated = updated + source
            made.append(updated.astype(jnp.bfloat16))
            new[b, band, here] = made[c]
        if last:
            if late:
                gathered = raw[b, :, here]
            else:
                gathered = from_snapshot(0, b, lambda c: lam[b, pl.ds(c * cells, cells), here])
            gathered = from_snapshot(1, b, lambda c: made[c], gathered)
            raw[b, :, here] = gathered
            square = gathered * gathered
            if counted is not None:
                square = square * counted
            summed[...] += sum(square[i : i + 8] for i in range(0, cells, 8))

    def picked(b, k, local=True, received=late):
        col = cols[b, k]
        nothing = jnp.zeros((rows, width), lam.dtype)
        block = nothing
        if received:
            block = jnp.where(col >= owned, slots[jnp.maximum(col - owned, 0)], nothing)
        if local:
            own = lam[jnp.clip(col, 0, owned - 1), :, here]
            block = jnp.where(jnp.logical_and(col >= 0, col < owned), own, block)
        return block

    def row_total(b, entries_of, **kinds):
        state = [
            lam[b, :, here] if k == 0 and kinds.get("local", True) else picked(b, k, **kinds)
            for k in entries_of
        ]
        weights = jnp.concatenate([ops[b, k] for k in entries_of], axis=1)
        return jnp.dot(
            weights, jnp.concatenate(state, axis=0), preferred_element_type=jnp.float32
        )

    def by_twos():
        for n in range(1, entries // 2 + 1):
            count = 0
            for b in range(owned):
                pairs, mine = shape_of(b)
                order[n - 1, count] = b
                count = count + jnp.logical_and(mine, pairs == n).astype(jnp.int32)

            @pl.loop(0, (count + 1) // 2)
            def _(i, n=n, count=count):
                b, other = order[n - 1, 2 * i], order[n - 1, jnp.minimum(2 * i + 1, count - 1)]
                if begin:
                    for p in range(n):
                        fetch(b, p).wait()

                    @pl.when(other != b)
                    def _():
                        for p in range(n):
                            fetch(other, p).wait()

                total, ahead = (row_total(i, range(2 * n)) for i in (b, other))
                finish(b, total)
                finish(other, ahead, jnp.where(other != b, 1.0, 0.0))

    plain = True
    for b in range(owned):
        pairs, mine = shape_of(b)
        plain = jnp.logical_and(plain, jnp.logical_and(mine == late, pairs == 1))

    if late:
        @pl.when(plain)
        def _():
            taken = (1,) if last else (0, 1)
            split = dict(local=not last)
            total = row_total(0, taken, **split)
            for b in range(owned):
                ahead = row_total(b + 1, taken, **split) if b + 1 < owned else None
                finish(b, total)
                total = ahead

        @pl.when(jnp.logical_not(plain))
        def _():
            by_twos()
    else:
        by_twos()

    if last and not late:

        @pl.when(plain)
        def _():
            for b in range(owned):
                prepare(b, row_total(b, (0,)))

        @pl.when(jnp.logical_not(plain))
        def _():
            @pl.loop(0, owned)
            def _(b):
                @pl.when(jnp.logical_not(shape_of(b)[1]))
                def _():
                    prepare(b, 0.0)

    if last:
        sums = jnp.sum(summed[...], axis=0, keepdims=True)[None]
        if late:
            squares[...] = jnp.broadcast_to(done_squares[...], squares.shape)
            sums = sums + done_squares[:, :, here]
        squares[:, :, here] = jnp.broadcast_to(sums, (squares.shape[0], 1, width))

    if begin:

        @pl.loop(0, owned)
        def _(b):
            @pl.when(jnp.logical_not(shape_of(b)[1]))
            def _():
                for_pairs(b, lambda copy: copy.wait())

    if sends:
        for r, c, row in sent_rows(ROUTES):
            sends[r][c] = new[row, :, here]


def step_rows(
    late, last, step, part, final, cost, inputs, lam, received=None, before=None, base=None
):
    cols, halo, ops, facts = inputs
    owned, rows, width = lam.shape
    cells = rows // 3
    devices = lax.axis_size("dom")
    smem, vmem = (pl.BlockSpec(memory_space=m) for m in (pltpu.SMEM, pltpu.VMEM))
    begin = not late and step == 0
    args = [in_hbm(cols) if begin else cols, halo, pinned(lam), in_hbm(ops) if begin else pinned(ops), *facts]
    aliases = {}
    if late:
        args += [pinned(received[r]) for r in ROUTES]
        for i in range(1 + last):
            aliases[len(args)] = i
            args.append(pinned(before[i]))
        if last:
            args += [before[2], pinned(base)]
    out_shape = [pltpu.VMEM(lam.shape, lam.dtype)]
    if last:
        out_shape += [
            pltpu.VMEM((owned, cells, width), jnp.float32),
            pltpu.VMEM((devices if final else 1, 1, width), jnp.float32),
        ]
        if not late:
            out_shape.append(pltpu.VMEM(lam.shape, jnp.float32))
    elif late:
        out_shape += [pltpu.VMEM((2, rows, part[1]), lam.dtype)] * 4
    scratch = [pltpu.SMEM((ops.shape[1] // 2, owned), jnp.int32)]
    if last:
        scratch += [pltpu.VMEM((8, part[1]), jnp.float32)]
    if late:
        scratch += [pltpu.VMEM((owned, rows, part[1]), lam.dtype)]
    if begin:
        scratch += [pltpu.SemaphoreType.DMA((owned, ops.shape[1] // 2))]
        out_shape += [
            pltpu.VMEM((owned, cells, 2 + 3 * 2), jnp.float32),
            pltpu.VMEM((4, width), jnp.float32),
            pltpu.VMEM(ops.shape, ops.dtype),
            pltpu.SMEM(cols.shape, cols.dtype),
            pltpu.SMEM(halo.shape, halo.dtype),
        ] + [pltpu.VMEM((2, rows, width // PARTS), lam.dtype)] * (3 * (PARTS - 1))
    return pl.pallas_call(
        functools.partial(step_kernel, late, last, step, part, final),
        name=("late" if late else "early") + "_rows",
        out_shape=out_shape,
        in_specs=[smem, smem, vmem, pl.BlockSpec(memory_space=pltpu.HBM) if begin else vmem]
        + [vmem] * (len(args) - 4),
        out_specs=[smem if o.memory_space == pltpu.SMEM else vmem for o in out_shape],
        input_output_aliases=aliases,
        scratch_shapes=scratch,
        compiler_params=pltpu.CompilerParams(vmem_limit_bytes=16 * 1024 * 1024),
        cost_estimate=pl.CostEstimate(flops=0, bytes_accessed=cost, transcendentals=0),
    )(*args)


def scale_kernel(cells_total, sums, raw, out, scaled_rows, sems):
    factor = lax.rsqrt(jnp.sum(sums[...], axis=0) / cells_total + 1e-06)
    copies = []
    for b in range(raw.shape[0]):
        scaled_rows[b] = raw[b] * factor
        copies.append(pltpu.make_async_copy(scaled_rows.at[b], out.at[b], sems.at[b]))
        copies[b].start()
    for copy in copies:
        copy.wait()


def scaled(sums, raw, cells_total):
    vmem = pl.BlockSpec(memory_space=pltpu.VMEM)
    return pl.pallas_call(
        functools.partial(scale_kernel, cells_total),
        name="scale",
        out_shape=jax.ShapeDtypeStruct(raw.shape, raw.dtype),
        in_specs=[vmem, vmem],
        out_specs=pl.BlockSpec(memory_space=pltpu.HBM),
        scratch_shapes=[
            pltpu.VMEM(raw.shape, raw.dtype),
            pltpu.SemaphoreType.DMA((raw.shape[0],)),
        ],
        compiler_params=pltpu.CompilerParams(vmem_limit_bytes=8 * 1024 * 1024),
    )(sums, pinned(raw))


def per_device(
    adjoint_end,
    operator_blocks,
    block_cols,
    halo_send,
    wet_cells,
    gauge_cells,
    window_first,
    window_len,
    gauge_gain,
    snapshots,
):
    owned, cells = wet_cells.shape
    steps = snapshots.shape[0]
    devices = lax.axis_size("dom")
    halo = jnp.swapaxes(halo_send, 1, 2)
    facts = [wet_cells, snapshots] + [
        v[None] for v in (gauge_cells, window_first, window_len, gauge_gain)
    ]
    width = adjoint_end.shape[2]
    parts = [(at, width // PARTS) for at in range(0, width, width // PARTS)]
    lam = adjoint_end
    received = [exchange(pick_sends(parts[0], PICK_COST, pltpu.HBM, halo, lam))]
    for step in range(steps):
        last = step == steps - 1
        inputs = (block_cols, halo, operator_blocks, facts)
        state = step_rows(False, last, step, (0, width), False, EARLY_COST, inputs, lam)
        base = None
        if last:
            *state, base = state
        if step == 0:
            state, (aux, gauges, *kept), picks = state[:1], state[1:6], state[6:]
            operator_blocks, block_cols, halo = kept
            received += [exchange(dict(zip(SPLIT, picks[i : i + 3]))) for i in range(0, len(picks), 3)]
            facts = [aux, gauges]
            inputs = (block_cols, halo, operator_blocks, facts)
        if step == 0:
            received[1:] = [some | {"swap": received[0]["swap"]} for some in received[1:]]
        arriving, received = received, []
        for i, part in enumerate(parts):
            final = last and i == len(parts) - 1
            state = step_rows(
                True, last, step, part, final, LATE_COST[step][i], inputs, lam, arriving[i], state, base
            )
            if not last:
                received.append(exchange(dict(zip(ROUTES, state[1:]))))
        lam = state[0]
    raw, squares = state[1:]
    sums = lax.all_to_all(squares, "dom", 0, 0, tiled=True)
    return (lam, scaled(sums, raw, devices * owned * cells))


def solution(mesh):
    return jax.shard_map(
        per_device,
        mesh=mesh,
        in_specs=(
            P("dom", None, None),
            P("dom", None, None, None),
            P("dom", None),
            P("dom", None, None),
            P("dom", None),
            P(),
            P(),
            P(),
            P(),
            P(None, "dom", None),
        ),
        out_specs=(P("dom", None, None), P("dom", None, None)),
        check_vma=False,
    )
```

profile of v0, /device:TPU:0, one launch (start us, length us, event | category | flops | bytes accessed | tf_op | source)
XLA Modules:
  0.0 74.7 jit_solution(2708276261547660499)
XLA Ops:
  0.7 2.2 %pick_sends.1 = (bf16[2,384,256]{2,1,0:T(8,128)(2,1)S(1)}, bf16[2,384,128]{2,1,0:T(8,128)(2,1)S(1)}, bf16[2,384,128]{2,1,0:T(8,128)(2,1)S(1)}, bf16[2,384,128]{2,1,0:T(8,128)(2,1)S(1)}) custom-call(s32[1,2,4]{2,1,0:T(2,128)} %bitcast.5, bf16[8,384,256]{2,1,0:T(8,128)(2,1)} %refs_2_.5), custom_call_target="tpu_custom_call" | custom-call | bytes 4194304 | tf_op jit(solution)/shard_map/pick_sends/pallas_call | solution.py:69
  2.9 0.5 collective-permute-start
  3.4 2.6 %collective-permute-start.4 = (bf16[2,384,128]{2,1,0:T(8,128)(2,1)S(1)}, bf16[2,384,128]{2,1,0:T(8,128)(2,1)S(1)}, u32[]{:S(2)}, u32[]{:S(2)}) collective-permute-start(bf16[2,384,128]{2,1,0:T(8,128)(2,1)S(1)} %get-tuple-element.44), channel_id=1, source_target_pairs={{0,2},{1,3},{2,0},{3,1},{4,6},{5,7},{6,4},{7,5},{8,10},{9,11},{10,... | collective-permute-start | bytes 589832 | tf_op jit(solution)/shard_map/ppermute | solution.py:40
  6.0 0.7 collective-permute-start.5
  6.6 0.7 collective-permute-start.6
  7.4 0.0 copy-start.1
  7.4 0.7 copy-done.1
  8.1 4.0 %early_rows.2 = (bf16[8,384,256]{2,1,0:T(8,128)(2,1)S(1)}, f32[8,128,8]{2,1,0:T(8,128)S(1)}, f32[4,256]{1,0:T(4,128)S(1)}, bf16[8,6,384,384]{3,2,1,0:T(8,128)(2,...) custom-call(s32[8,6]{1,0:T(8,128)} %refs_0_.1, ...), custom_call_target="tpu_custom_call" | custom-call | bytes 4194304 | tf_op jit(solution)/shard_map/early_rows/pallas_call | solution.py:372
  12.1 5.2 %collective-permute-start.1 = (bf16[2,384,128]{2,1,0:T(8,128)(2,1)S(1)}, bf16[2,384,128]{2,1,0:T(8,128)(2,1)S(1)}, u32[]{:S(2)}, u32[]{:S(2)}) collective-permute-start(bf16[2,384,128]{2,1,0:T(8,128)(2,1)S(1)} %get-tuple-element.41), channel_id=1, source_target_pairs={{0,2},{1,3},{2,0},{3,1},{4,6},{5,7},{6,4},{7,5},{8,10},{9,11},{10,... | collective-permute-start | bytes 589832 | tf_op jit(solution)/shard_map/ppermute | solution.py:40
  17.3 0.7 collective-permute-start.2
  18.0 0.0 collective-permute-done.5.refs_8_
  18.0 0.7 collective-permute-start.3
  18.7 0.0 collective-permute-done.6.refs_9_
  18.7 1.7 %late_rows.4 = (bf16[8,384,256]{2,1,0:T(8,128)(2,1)S(1)}, bf16[2,384,128]{2,1,0:T(8,128)(2,1)S(1)}, bf16[2,384,128]{2,1,0:T(8,128)(2,1)S(1)}, bf16[2,384,128]{2,1,0:T(8,128)(2,1)S(1)}, bf16[2,384,128]{2,1,0:T(8,128)(2,1)S(1)}) custom-call(s32[8,6]{1,0:T(8,128)S(4)} %get-tuple-element.35.refs_0_, ...), custom_call_target="tpu_custom_call", output_to_operand_aliasing={{0}: (10, {})} | custom-call | bytes 4194304 | tf_op jit(solution)/shard_map/late_rows/pallas_call | solution.py:372
  20.5 5.8 %collective-permute-start.11 = (bf16[2,384,128]{2,1,0:T(8,128)(2,1)S(1)}, bf16[2,384,128]{2,1,0:T(8,128)(2,1)S(1)}, u32[]{:S(2)}, u32[]{:S(2)}) collective-permute-start(bf16[2,384,128]{2,1,0:T(8,128)(2,1)S(1)} %get-tuple-element.54), channel_id=1, source_target_pairs={{0,1},{1,0},{2,3},{3,2},{4,5},{5,4},{6,7},{7,6},{8,9},{9,8},{10,11... | collective-permute-start | bytes 589832 | tf_op jit(solution)/shard_map/ppermute | solution.py:40
  26.3 1.8 %collective-permute-start.12 = (bf16[2,384,128]{2,1,0:T(8,128)(2,1)S(1)}, bf16[2,384,128]{2,1,0:T(8,128)(2,1)S(1)}, u32[]{:S(2)}, u32[]{:S(2)}) collective-permute-start(bf16[2,384,128]{2,1,0:T(8,128)(2,1)S(1)} %get-tuple-element.55), channel_id=1, source_target_pairs={{0,2},{1,3},{2,0},{3,1},{4,6},{5,7},{6,4},{7,5},{8,10},{9,11},{10,... | collective-permute-start | bytes 589832 | tf_op jit(solution)/shard_map/ppermute | solution.py:40
  28.1 0.7 collective-permute-start.13
  28.7 0.0 collective-permute-done.3.refs_9_
  28.8 1.9 %late_rows.5 = (bf16[8,384,256]{2,1,0:T(8,128)(2,1)S(1)}, bf16[2,384,128]{2,1,0:T(8,128)(2,1)S(1)}, bf16[2,384,128]{2,1,0:T(8,128)(2,1)S(1)}, bf16[2,384,128]{2,1,0:T(8,128)(2,1)S(1)}, bf16[2,384,128]{2,1,0:T(8,128)(2,1)S(1)}) custom-call(s32[8,6]{1,0:T(8,128)S(4)} %get-tuple-element.35.refs_0_, ...), custom_call_target="tpu_custom_call", output_to_operand_aliasing={{0}: (10, {})} | custom-call | bytes 4194304 | tf_op jit(solution)/shard_map/late_rows/pallas_call | solution.py:372
  30.7 5.5 %collective-permute-start.7 = (bf16[2,384,128]{2,1,0:T(8,128)(2,1)S(1)}, bf16[2,384,128]{2,1,0:T(8,128)(2,1)S(1)}, u32[]{:S(2)}, u32[]{:S(2)}) collective-permute-start(bf16[2,384,128]{2,1,0:T(8,128)(2,1)S(1)} %get-tuple-element.50), channel_id=1, source_target_pairs={{0,1},{1,0},{2,3},{3,2},{4,5},{5,4},{6,7},{7,6},{8,9},{9,8},{10,11... | collective-permute-start | bytes 589832 | tf_op jit(solution)/shard_map/ppermute | solution.py:40
  36.2 0.7 collective-permute-start.14
  36.9 3.6 %collective-permute-start.8 = (bf16[2,384,128]{2,1,0:T(8,128)(2,1)S(1)}, bf16[2,384,128]{2,1,0:T(8,128)(2,1)S(1)}, u32[]{:S(2)}, u32[]{:S(2)}) collective-permute-start(bf16[2,384,128]{2,1,0:T(8,128)(2,1)S(1)} %get-tuple-element.51), channel_id=1, source_target_pairs={{0,2},{1,3},{2,0},{3,1},{4,6},{5,7},{6,4},{7,5},{8,10},{9,11},{10,... | collective-permute-start | bytes 589832 | tf_op jit(solution)/shard_map/ppermute | solution.py:40
  40.5 0.7 collective-permute-start.9
  41.2 0.7 collective-permute-start.10
  41.9 2.5 %early_rows.3 = (bf16[8,384,256]{2,1,0:T(8,128)(2,1)S(1)}, f32[8,128,256]{2,1,0:T(8,128)S(1)}, f32[1,1,256]{2,1,0:T(1,128)S(1)}, f32[8,384,256]{2,1,0:T(8,128)S(1)}) custom-call(s32[8,6]{1,0:T(8,128)S(4)} %get-tuple-element.35.refs_0_, s32[1,2,4]{2,1,0:T(2,128)S(4)} %get-tuple-element.36.refs_1_, bf16[8,384,256]{2,1,0:T(8,128)(2,1)S(1)} %get-tuple-element.49.refs_2_, ...), custom_call_target="tpu_custom_call" | custom-call | bytes 4194304 | tf_op jit(solution)/shard_map/early_rows/pallas_call | solution.py:372
  44.4 1.6 %late_rows.6 = (bf16[8,384,256]{2,1,0:T(8,128)(2,1)S(1)}, f32[8,128,256]{2,1,0:T(8,128)S(1)}, f32[1,1,256]{2,1,0:T(1,128)S(1)}) custom-call(s32[8,6]{1,0:T(8,128)S(4)} %get-tuple-element.35.refs_0_, s32[1,2,4]{2,1,0:T(2,128)S(4)} %get-tuple-element.36.refs_1_, ...), custom_call_target="tpu_custom_call", output_to_operand_aliasing={{0}: (10, {}), {1}: (11, {})} | custom-call | bytes 4194304 | tf_op jit(solution)/shard_map/late_rows/pallas_call | solution.py:372
  46.0 5.9 %collective-permute-done.8.refs_7_ = bf16[2,384,128]{2,1,0:T(8,128)(2,1)S(1)} collective-permute-done((bf16[2,384,128]{2,1,0:T(8,128)(2,1)S(1)}, bf16[2,384,128]{2,1,0:T(8,128)(2,1)S(1)}, u32[]{:S(2)}, u32[]{:S(2)}) %collective-permute-start.8) | collective-permute-done | bytes 196640 | tf_op jit(solution)/shard_map/ppermute | solution.py:40
  51.9 2.2 %late_rows.7 = (bf16[8,384,256]{2,1,0:T(8,128)(2,1)S(1)}, f32[8,128,256]{2,1,0:T(8,128)S(1)}, f32[32,1,256]{2,1,0:T(1,128)}) custom-call(s32[8,6]{1,0:T(8,128)S(4)} %get-tuple-element.35.refs_0_, s32[1,2,4]{2,1,0:T(2,128)S(4)} %get-tuple-element.36.refs_1_, ...), custom_call_target="tpu_custom_call", output_to_operand_aliasing={{0}: (10, {}), {1}: (11, {})} | custom-call | bytes 4194304 | tf_op jit(solution)/shard_map/late_rows/pallas_call | solution.py:372
  54.2 12.0 %all-to-all-start = ((f32[32,1,256]{2,1,0:T(1,128)}), f32[32,1,256]{2,1,0:T(1,128)S(1)}, u32[]{:S(2)}, u32[]{:S(2)}) async-start(f32[32,1,256]{2,1,0:T(1,128)} %get-tuple-element.66), calls=%async_computation | async-start | bytes 65536 | tf_op jit(solution)/shard_map/all_to_all | solution.py:461
  66.2 1.1 %copy.24 = bf16[8,384,256]{2,1,0:T(8,128)(2,1)} copy(bf16[8,384,256]{2,1,0:T(8,128)(2,1)S(1)} %get-tuple-element.68) | data formatting | bytes 3145728
  67.3 6.1 %all-to-all-done.sums = f32[32,1,256]{2,1,0:T(1,128)S(1)} async-done(((f32[32,1,256]{2,1,0:T(1,128)}), f32[32,1,256]{2,1,0:T(1,128)S(1)}, u32[]{:S(2)}, u32[]{:S(2)}) %all-to-all-start) | async-done | bytes 32800 | tf_op jit(solution)/shard_map/all_to_all | solution.py:461
  73.4 1.1 %scale.1 = f32[8,128,256]{2,1,0:T(8,128)} custom-call(f32[32,1,256]{2,1,0:T(1,128)S(1)} %all-to-all-done.sums, f32[8,128,256]{2,1,0:T(8,128)S(1)} %get-tuple-element.67.raw), custom_call_target="tpu_custom_call" | custom-call | tf_op jit(solution)/shard_map/scale/pallas_call | solution.py:399
  (25 shorter events, 0.1 us)
Async XLA Ops:
  0.6 6.7 %copy-start = (bf16[8,384,256]{2,1,0:T(8,128)(2,1)S(1)}, bf16[8,384,256]{2,1,0:T(8,128)(2,1)}, u32[]{:S(2)}) copy-start(bf16[8,384,256]{2,1,0:T(8,128)(2,1)} %refs_2_.5) | copy-start | bytes 4718596
  0.6 6.7 %copy-start.3 = (s32[1,4,2]{1,2,0:T(2,128)S(1)}, s32[1,4,2]{1,2,0:T(2,128)}, u32[]{:S(2)}) copy-start(s32[1,4,2]{1,2,0:T(2,128)} %param.13) | copy-start | bytes 100
  0.7 6.7 %copy-start.7 = (f32[256]{0:T(256)S(1)}, f32[256]{0:T(256)}, u32[]{:S(2)}) copy-start(f32[256]{0:T(256)} %param.18) | copy-start | bytes 3076
  0.7 6.7 %copy-start.6 = (s32[256]{0:T(256)S(1)}, s32[256]{0:T(256)}, u32[]{:S(2)}) copy-start(s32[256]{0:T(256)} %param.17) | copy-start | bytes 3076
  0.7 6.7 %copy-start.5 = (s32[256]{0:T(256)S(1)}, s32[256]{0:T(256)}, u32[]{:S(2)}) copy-start(s32[256]{0:T(256)} %param.16) | copy-start | bytes 3076
  0.7 6.7 %copy-start.4 = (s32[256]{0:T(256)S(1)}, s32[256]{0:T(256)}, u32[]{:S(2)}) copy-start(s32[256]{0:T(256)} %param.15) | copy-start | bytes 3076
  0.7 6.7 %copy-start.2 = (s32[8,128]{1,0:T(8,128)S(1)}, s32[8,128]{1,0:T(8,128)}, u32[]{:S(2)}) copy-start(s32[8,128]{1,0:T(8,128)} %refs_4_.1) | copy-start | bytes 12292
  2.9 15.8 %collective-permute-start = (bf16[2,384,256]{2,1,0:T(8,128)(2,1)S(1)}, bf16[2,384,256]{2,1,0:T(8,128)(2,1)S(1)}, u32[]{:S(2)}, u32[]{:S(2)}) collective-permute-start(bf16[2,384,256]{2,1,0:T(8,128)(2,1)S(1)} %get-tuple-element.40), channel_id=1, source_target_pairs={{0,1},{1,0},{2,3},{3,2},{4,5},{5,4},{6,7},{7,6},{8,9},{9,8},{10,11... | collective-permute-start | bytes 1179656 | tf_op jit(solution)/shard_map/ppermute | solution.py:40
  3.4 13.9 %collective-permute-start.4 = (bf16[2,384,128]{2,1,0:T(8,128)(2,1)S(1)}, bf16[2,384,128]{2,1,0:T(8,128)(2,1)S(1)}, u32[]{:S(2)}, u32[]{:S(2)}) collective-permute-start(bf16[2,384,128]{2,1,0:T(8,128)(2,1)S(1)} %get-tuple-element.44), channel_id=1, source_target_pairs={{0,2},{1,3},{2,0},{3,1},{4,6},{5,7},{6,4},{7,5},{8,10},{9,11},{10,... | collective-permute-start | bytes 589832 | tf_op jit(solution)/shard_map/ppermute | solution.py:40
  6.0 12.0 %collective-permute-start.5 = (bf16[2,384,128]{2,1,0:T(8,128)(2,1)S(1)}, bf16[2,384,128]{2,1,0:T(8,128)(2,1)S(1)}, u32[]{:S(2)}, u32[]{:S(2)}) collective-permute-start(bf16[2,384,128]{2,1,0:T(8,128)(2,1)S(1)} %get-tuple-element.45), channel_id=1, source_target_pairs={{2,4},{3,5},{6,8},{7,9},{10,12},{11,13},{14,16},{15,17},{18,20},{1... | collective-permute-start | bytes 589832 | tf_op jit(solution)/shard_map/ppermute | solution.py:40
  6.6 12.0 %collective-permute-start.6 = (bf16[2,384,128]{2,1,0:T(8,128)(2,1)S(1)}, bf16[2,384,128]{2,1,0:T(8,128)(2,1)S(1)}, u32[]{:S(2)}, u32[]{:S(2)}) collective-permute-start(bf16[2,384,128]{2,1,0:T(8,128)(2,1)S(1)} %get-tuple-element.46), channel_id=1, source_target_pairs={{1,2},{3,4},{5,6},{7,8},{9,10},{11,12},{13,14},{15,16},{17,18},{19... | collective-permute-start | bytes 589832 | tf_op jit(solution)/shard_map/ppermute | solution.py:40
  7.4 0.7 copy-start.1
  12.1 16.0 %collective-permute-start.1 = (bf16[2,384,128]{2,1,0:T(8,128)(2,1)S(1)}, bf16[2,384,128]{2,1,0:T(8,128)(2,1)S(1)}, u32[]{:S(2)}, u32[]{:S(2)}) collective-permute-start(bf16[2,384,128]{2,1,0:T(8,128)(2,1)S(1)} %get-tuple-element.41), channel_id=1, source_target_pairs={{0,2},{1,3},{2,0},{3,1},{4,6},{5,7},{6,4},{7,5},{8,10},{9,11},{10,... | collective-permute-start | bytes 589832 | tf_op jit(solution)/shard_map/ppermute | solution.py:40
  17.3 11.4 %collective-permute-start.2 = (bf16[2,384,128]{2,1,0:T(8,128)(2,1)S(1)}, bf16[2,384,128]{2,1,0:T(8,128)(2,1)S(1)}, u32[]{:S(2)}, u32[]{:S(2)}) collective-permute-start(bf16[2,384,128]{2,1,0:T(8,128)(2,1)S(1)} %get-tuple-element.42), channel_id=1, source_target_pairs={{2,4},{3,5},{6,8},{7,9},{10,12},{11,13},{14,16},{15,17},{18,20},{1... | collective-permute-start | bytes 589832 | tf_op jit(solution)/shard_map/ppermute | solution.py:40
  18.0 10.7 %collective-permute-start.3 = (bf16[2,384,128]{2,1,0:T(8,128)(2,1)S(1)}, bf16[2,384,128]{2,1,0:T(8,128)(2,1)S(1)}, u32[]{:S(2)}, u32[]{:S(2)}) collective-permute-start(bf16[2,384,128]{2,1,0:T(8,128)(2,1)S(1)} %get-tuple-element.43), channel_id=1, source_target_pairs={{1,2},{3,4},{5,6},{7,8},{9,10},{11,12},{13,14},{15,16},{17,18},{19... | collective-permute-start | bytes 589832 | tf_op jit(solution)/shard_map/ppermute | solution.py:40
  20.5 16.4 %collective-permute-start.11 = (bf16[2,384,128]{2,1,0:T(8,128)(2,1)S(1)}, bf16[2,384,128]{2,1,0:T(8,128)(2,1)S(1)}, u32[]{:S(2)}, u32[]{:S(2)}) collective-permute-start(bf16[2,384,128]{2,1,0:T(8,128)(2,1)S(1)} %get-tuple-element.54), channel_id=1, source_target_pairs={{0,1},{1,0},{2,3},{3,2},{4,5},{5,4},{6,7},{7,6},{8,9},{9,8},{10,11... | collective-permute-start | bytes 589832 | tf_op jit(solution)/shard_map/ppermute | solution.py:40
  26.3 14.2 %collective-permute-start.12 = (bf16[2,384,128]{2,1,0:T(8,128)(2,1)S(1)}, bf16[2,384,128]{2,1,0:T(8,128)(2,1)S(1)}, u32[]{:S(2)}, u32[]{:S(2)}) collective-permute-start(bf16[2,384,128]{2,1,0:T(8,128)(2,1)S(1)} %get-tuple-element.55), channel_id=1, source_target_pairs={{0,2},{1,3},{2,0},{3,1},{4,6},{5,7},{6,4},{7,5},{8,10},{9,11},{10,... | collective-permute-start | bytes 589832 | tf_op jit(solution)/shard_map/ppermute | solution.py:40
  28.1 13.1 %collective-permute-start.13 = (bf16[2,384,128]{2,1,0:T(8,128)(2,1)S(1)}, bf16[2,384,128]{2,1,0:T(8,128)(2,1)S(1)}, u32[]{:S(2)}, u32[]{:S(2)}) collective-permute-start(bf16[2,384,128]{2,1,0:T(8,128)(2,1)S(1)} %get-tuple-element.56), channel_id=1, source_target_pairs={{2,4},{3,5},{6,8},{7,9},{10,12},{11,13},{14,16},{15,17},{18,20},{1... | collective-permute-start | bytes 589832 | tf_op jit(solution)/shard_map/ppermute | solution.py:40
  30.7 15.3 %collective-permute-start.7 = (bf16[2,384,128]{2,1,0:T(8,128)(2,1)S(1)}, bf16[2,384,128]{2,1,0:T(8,128)(2,1)S(1)}, u32[]{:S(2)}, u32[]{:S(2)}) collective-permute-start(bf16[2,384,128]{2,1,0:T(8,128)(2,1)S(1)} %get-tuple-element.50), channel_id=1, source_target_pairs={{0,1},{1,0},{2,3},{3,2},{4,5},{5,4},{6,7},{7,6},{8,9},{9,8},{10,11... | collective-permute-start | bytes 589832 | tf_op jit(solution)/shard_map/ppermute | solution.py:40
  36.2 8.2 %collective-permute-start.14 = (bf16[2,384,128]{2,1,0:T(8,128)(2,1)S(1)}, bf16[2,384,128]{2,1,0:T(8,128)(2,1)S(1)}, u32[]{:S(2)}, u32[]{:S(2)}) collective-permute-start(bf16[2,384,128]{2,1,0:T(8,128)(2,1)S(1)} %get-tuple-element.57), channel_id=1, source_target_pairs={{1,2},{3,4},{5,6},{7,8},{9,10},{11,12},{13,14},{15,16},{17,18},{19... | collective-permute-start | bytes 589832 | tf_op jit(solution)/shard_map/ppermute | solution.py:40
  36.9 15.0 %collective-permute-start.8 = (bf16[2,384,128]{2,1,0:T(8,128)(2,1)S(1)}, bf16[2,384,128]{2,1,0:T(8,128)(2,1)S(1)}, u32[]{:S(2)}, u32[]{:S(2)}) collective-permute-start(bf16[2,384,128]{2,1,0:T(8,128)(2,1)S(1)} %get-tuple-element.51), channel_id=1, source_target_pairs={{0,2},{1,3},{2,0},{3,1},{4,6},{5,7},{6,4},{7,5},{8,10},{9,11},{10,... | collective-permute-start | bytes 589832 | tf_op jit(solution)/shard_map/ppermute | solution.py:40
  40.5 11.4 %collective-permute-start.9 = (bf16[2,384,128]{2,1,0:T(8,128)(2,1)S(1)}, bf16[2,384,128]{2,1,0:T(8,128)(2,1)S(1)}, u32[]{:S(2)}, u32[]{:S(2)}) collective-permute-start(bf16[2,384,128]{2,1,0:T(8,128)(2,1)S(1)} %get-tuple-element.52), channel_id=1, source_target_pairs={{2,4},{3,5},{6,8},{7,9},{10,12},{11,13},{14,16},{15,17},{18,20},{1... | collective-permute-start | bytes 589832 | tf_op jit(solution)/shard_map/ppermute | solution.py:40
  41.2 10.7 %collective-permute-start.10 = (bf16[2,384,128]{2,1,0:T(8,128)(2,1)S(1)}, bf16[2,384,128]{2,1,0:T(8,128)(2,1)S(1)}, u32[]{:S(2)}, u32[]{:S(2)}) collective-permute-start(bf16[2,384,128]{2,1,0:T(8,128)(2,1)S(1)} %get-tuple-element.53), channel_id=1, source_target_pairs={{1,2},{3,4},{5,6},{7,8},{9,10},{11,12},{13,14},{15,16},{17,18},{19... | collective-permute-start | bytes 589832 | tf_op jit(solution)/shard_map/ppermute | solution.py:40
  54.2 19.3 %all-to-all-start = ((f32[32,1,256]{2,1,0:T(1,128)}), f32[32,1,256]{2,1,0:T(1,128)S(1)}, u32[]{:S(2)}, u32[]{:S(2)}) async-start(f32[32,1,256]{2,1,0:T(1,128)} %get-tuple-element.66), calls=%async_computation | async-start | bytes 65536 | tf_op jit(solution)/shard_map/all_to_all | solution.py:461
where the time goes:
time: 76.2 us; the launch traced here: 74.7 us
  starting transfers between devices  42.4 us (56%)
  Pallas kernels  17.3 us (23%)
  waiting for transfers between devices  12 us (16%)
  local copies, waits for them, and re-layouts  1.91 us (3%)
  between operations  1.1 us (1%)
    ppermute x15, starting transfers between devices, exchange(): return {r: lax.ppermute(sent, 'dom', pairs[r]) for r, sent in sends.items()}  30.4 us
    pallas_call x6, Pallas kernels, step_rows(): pl.pallas_call(functools.partial(step_kernel, late, last, step, part, fin...  14 us
    all_to_all x1, starting transfers between devices, per_device(): sums = lax.all_to_all(squares, 'dom', 0, 0, tiled=True)  12 us
    all_to_all x1, waiting for transfers between devices, per_device(): sums = lax.all_to_all(squares, 'dom', 0, 0, tiled=True)  6.1 us
    ppermute x15, waiting for transfers between devices, exchange(): return {r: lax.ppermute(sent, 'dom', pairs[r]) for r, sent in sends.items()}  5.92 us
    pallas_call x1, Pallas kernels, pick_sends(): pl.pallas_call(functools.partial(pick_kernel, part), name='pick_sends', o...  2.18 us
    unnamed x17, local copies, waits for them, and re-layouts  1.91 us
  transfers between devices with their start and end apart: 16, of which 2 were waited for; matrix products, arithmetic and copies ran while one was open for 2% of the time, Pallas kernels for 16%

commit v1 on v0

--- a/solution.py
+++ b/solution.py
@@ -11,9 +11,7 @@
 PICK_COST = 4 << 20
 EARLY_COST = 4 << 20
 LATE_COST = ((4 << 20, 4 << 20), (4 << 20, 4 << 20))
-SPLIT = ("inner", "outer", "cross")
-FIRST = ("swap",) + SPLIT
-ROUTES = ("swap",) + SPLIT
+ROUTES = ("inner", "outer", "cross", "swap")
 
 
 def route_pairs(devices):
@@ -37,7 +35,7 @@
 
 def exchange(sends):
     pairs = route_pairs(lax.axis_size("dom"))
-    return {r: lax.ppermute(sent, "dom", pairs[r]) for r, sent in sends.items()}
+    return {r: lax.ppermute(sends[r], "dom", pairs[r]) for r in ROUTES}
 
 
 def pinned(value):
@@ -49,15 +47,14 @@
 
 
 def pick_kernel(part, halo, lam, *rest):
-    outs, sems = dict(zip(FIRST, rest[:4])), rest[4]
+    outs, sems = dict(zip(ROUTES, rest[:4])), rest[4]
     groups = send_groups(lax.axis_index("dom"))
     copies = []
-    for i, r in enumerate(FIRST):
-        band = pl.ds(*(part if r in SPLIT else (0, lam.shape[2])))
+    for i, r in enumerate(ROUTES):
         for c in range(2):
             row = jnp.maximum(halo[0, c, groups[r]], 0)
             copies.append(
-                pltpu.make_async_copy(lam.at[row, :, band], outs[r].at[c], sems.at[i, c])
+                pltpu.make_async_copy(lam.at[row, :, pl.ds(*part)], outs[r].at[c], sems.at[i, c])
             )
     for copy in copies:
         copy.start()
@@ -66,20 +63,18 @@
 
 
 def pick_sends(part, cost, place, halo, lam):
+    sent = pltpu.VMEM((2, lam.shape[1], part[1]), lam.dtype)
     outs = pl.pallas_call(
         functools.partial(pick_kernel, part),
         name="pick_sends",
-        out_shape=[
-            pltpu.VMEM((2, lam.shape[1], part[1] if r in SPLIT else lam.shape[2]), lam.dtype)
-            for r in FIRST
-        ],
+        out_shape=[sent] * 4,
         in_specs=[pl.BlockSpec(memory_space=pltpu.SMEM), pl.BlockSpec(memory_space=place)],
         out_specs=[pl.BlockSpec(memory_space=pltpu.VMEM)] * 4,
         scratch_shapes=[pltpu.SemaphoreType.DMA((4, 2))],
         compiler_params=pltpu.CompilerParams(vmem_limit_bytes=4 * 1024 * 1024),
         cost_estimate=pl.CostEstimate(flops=0, bytes_accessed=cost, transcendentals=0),
     )(in_hbm(halo), pltpu.with_memory_space_constraint(lam, place))
-    return dict(zip(FIRST, outs))
+    return dict(zip(ROUTES, outs))
 
 
 def lay_out_facts(facts, aux, gauges):
@@ -103,7 +98,7 @@
     begin = not late and step == 0
     facts = take(6) if begin else None
     aux, gauges = (None, None) if begin else take(2)
-    received = dict(zip(ROUTES, take(4))) if late else {}
+    received = take(4) if late else []
     take(1 + last if late else 0)
     done_squares = take(1)[0] if late and last else None
     base = take(1)[0] if late and last else None
@@ -113,7 +108,7 @@
     sends = dict(zip(ROUTES, take(4))) if late and not last else {}
     if begin:
         aux, gauges, kept, kept_cols, kept_halo = take(5)
-        ahead = [dict(zip(SPLIT, take(3))) for _ in range(PARTS - 1)]
+        ahead = [dict(zip(ROUTES, take(4))) for _ in range(PARTS - 1)]
         far, ops = ops, kept
     order = refs.pop(0)
     summed = refs.pop(0) if last else None
@@ -126,16 +121,14 @@
     here = pl.ds(*part)
     position = lax.axis_index("dom")
 
-    def sent_rows(routes):
+    def sent_rows():
         groups = send_groups(position)
-        return [(r, c, jnp.maximum(halo[0, c, groups[r]], 0)) for r in routes for c in range(2)]
+        return [(r, c, jnp.maximum(halo[0, c, groups[r]], 0)) for r in ROUTES for c in range(2)]
 
     if late:
         groups = receive_groups(position)
-        for r in ROUTES:
-            slots[pl.ds(2 * groups[r], 2)] = (
-                received[r][:, :, here] if r == "swap" and step == 0 else received[r][...]
-            )
+        for i, r in enumerate(ROUTES):
+            slots[pl.ds(2 * groups[r], 2)] = received[i][...]
     if last:
         summed[...] = jnp.zeros(summed.shape, jnp.float32)
 
@@ -177,7 +170,7 @@
                 kept_halo[0, c, o] = halo[0, c, o]
         for i, picks in enumerate(ahead):
             band = pl.ds((i + 1) * (part[1] // PARTS), part[1] // PARTS)
-            for r, c, row in sent_rows(SPLIT):
+            for r, c, row in sent_rows():
                 picks[r][c] = lam[row, :, band]
 
     first = gauges[1:2, here]
@@ -323,7 +316,7 @@
                 for_pairs(b, lambda copy: copy.wait())
 
     if sends:
-        for r, c, row in sent_rows(ROUTES):
+        for r, c, row in sent_rows():
             sends[r][c] = new[row, :, here]
 
 
@@ -368,7 +361,7 @@
             pltpu.VMEM(ops.shape, ops.dtype),
             pltpu.SMEM(cols.shape, cols.dtype),
             pltpu.SMEM(halo.shape, halo.dtype),
-        ] + [pltpu.VMEM((2, rows, width // PARTS), lam.dtype)] * (3 * (PARTS - 1))
+        ] + [pltpu.VMEM((2, rows, width // PARTS), lam.dtype)] * (4 * (PARTS - 1))
     return pl.pallas_call(
         functools.partial(step_kernel, late, last, step, part, final),
         name=("late" if late else "early") + "_rows",
@@ -443,11 +436,9 @@
         if step == 0:
             state, (aux, gauges, *kept), picks = state[:1], state[1:6], state[6:]
             operator_blocks, block_cols, halo = kept
-            received += [exchange(dict(zip(SPLIT, picks[i : i + 3]))) for i in range(0, len(picks), 3)]
+            received += [exchange(dict(zip(ROUTES, picks[i : i + 4]))) for i in range(0, len(picks), 4)]
             facts = [aux, gauges]
             inputs = (block_cols, halo, operator_blocks, facts)
-        if step == 0:
-            received[1:] = [some | {"swap": received[0]["swap"]} for some in received[1:]]
         arriving, received = received, []
         for i, part in enumerate(parts):
             final = last and i == len(parts) - 1

time: 76.2 us -> 76.6 us (level); the launches traced: 74.7 us -> 76.7 us
  starting transfers between devices: 42.4 us -> 50.6 us
  waiting for transfers between devices: 12 us -> 6.15 us
    ppermute x15 -> x16, starting transfers between devices: 30.4 us -> 41.2 us  [exchange(): return {r: lax.ppermute(sends[r], 'dom', pairs[r]) for r in ROUTES}]
    ppermute x15 -> x16, waiting for transfers between devices: 5.92 us -> 0.04 us  [exchange(): return {r: lax.ppermute(sends[r], 'dom', pairs[r]) for r in ROUTES}]
    all_to_all x1, starting transfers between devices: 12 us -> 9.36 us  [per_device(): sums = lax.all_to_all(squares, 'dom', 0, 0, tiled=True)]
  transfers between devices with their start and end apart: 16 -> 17, of which waited for: 2 -> 1; matrix products, arithmetic and copies ran while one was open for 2% -> 1% of each run, Pallas kernels for 16% -> 15%
where the time goes in v1:
time: 76.6 us; the launch traced here: 76.7 us
  starting transfers between devices  50.6 us (66%)
  Pallas kernels  17 us (22%)
  waiting for transfers between devices  6.15 us (8%)
  local copies, waits for them, and re-layouts  1.91 us (2%)
  between operations  1.11 us (1%)
    ppermute x16, starting transfers between devices, exchange(): return {r: lax.ppermute(sends[r], 'dom', pairs[r]) for r in ROUTES}  41.2 us
    pallas_call x6, Pallas kernels, step_rows(): pl.pallas_call(functools.partial(step_kernel, late, last, step, part, fin...  13.8 us
    all_to_all x1, starting transfers between devices, per_device(): sums = lax.all_to_all(squares, 'dom', 0, 0, tiled=True)  9.36 us
    all_to_all x1, waiting for transfers between devices, per_device(): sums = lax.all_to_all(squares, 'dom', 0, 0, tiled=True)  6.1 us
    pallas_call x1, Pallas kernels, pick_sends(): pl.pallas_call(functools.partial(pick_kernel, part), name='pick_sends', o...  2.13 us
    unnamed x17, local copies, waits for them, and re-layouts  1.91 us
  transfers between devices with their start and end apart: 17, of which 1 were waited for; matrix products, arithmetic and copies ran while one was open for 1% of the time, Pallas kernels for 15%

profile of v1, /device:TPU:0, one launch (start us, length us, event | category | flops | bytes accessed | tf_op | source)
XLA Modules:
  0.0 76.7 jit_solution(13818570676697531951)
XLA Ops:
  0.7 2.1 %pick_sends.1 = (bf16[2,384,128]{2,1,0:T(8,128)(2,1)S(1)}, bf16[2,384,128]{2,1,0:T(8,128)(2,1)S(1)}, bf16[2,384,128]{2,1,0:T(8,128)(2,1)S(1)}, bf16[2,384,128]{2,1,0:T(8,128)(2,1)S(1)}) custom-call(s32[1,2,4]{2,1,0:T(2,128)} %bitcast.5, bf16[8,384,256]{2,1,0:T(8,128)(2,1)} %refs_2_.5), custom_call_target="tpu_custom_call" | custom-call | bytes 4194304 | tf_op jit(solution)/shard_map/pick_sends/pallas_call | solution.py:67
  2.8 3.0 %collective-permute-start.4 = (bf16[2,384,128]{2,1,0:T(8,128)(2,1)S(1)}, bf16[2,384,128]{2,1,0:T(8,128)(2,1)S(1)}, u32[]{:S(2)}, u32[]{:S(2)}) collective-permute-start(bf16[2,384,128]{2,1,0:T(8,128)(2,1)S(1)} %get-tuple-element.45), channel_id=1, source_target_pairs={{0,2},{1,3},{2,0},{3,1},{4,6},{5,7},{6,4},{7,5},{8,10},{9,11},{10,... | collective-permute-start | bytes 589832 | tf_op jit(solution)/shard_map/ppermute | solution.py:38
  5.8 0.7 collective-permute-start.5
  6.5 0.7 collective-permute-start.6
  7.2 5.6 %collective-permute-start.7 = (bf16[2,384,128]{2,1,0:T(8,128)(2,1)S(1)}, bf16[2,384,128]{2,1,0:T(8,128)(2,1)S(1)}, u32[]{:S(2)}, u32[]{:S(2)}) collective-permute-start(bf16[2,384,128]{2,1,0:T(8,128)(2,1)S(1)} %get-tuple-element.48), channel_id=1, source_target_pairs={{0,1},{1,0},{2,3},{3,2},{4,5},{5,4},{6,7},{7,6},{8,9},{9,8},{10,11... | collective-permute-start | bytes 589832 | tf_op jit(solution)/shard_map/ppermute | solution.py:38
  12.9 0.0 copy-start.1
  12.9 0.7 copy-done.1
  13.6 4.0 %early_rows.2 = (bf16[8,384,256]{2,1,0:T(8,128)(2,1)S(1)}, f32[8,128,8]{2,1,0:T(8,128)S(1)}, f32[4,256]{1,0:T(4,128)S(1)}, bf16[8,6,384,384]{3,2,1,0:T(8,128)(2,...) custom-call(s32[8,6]{1,0:T(8,128)} %refs_0_.1, ...), custom_call_target="tpu_custom_call" | custom-call | bytes 4194304 | tf_op jit(solution)/shard_map/early_rows/pallas_call | solution.py:365
  17.6 0.1 collective-permute-start
  17.7 0.0 collective-permute-done.4.refs_6_
  17.7 0.7 collective-permute-start.1
  18.3 0.0 collective-permute-done.5.refs_7_
  18.4 0.7 collective-permute-start.2
  19.0 0.0 collective-permute-done.6.refs_8_
  19.0 9.8 %collective-permute-start.3 = (bf16[2,384,128]{2,1,0:T(8,128)(2,1)S(1)}, bf16[2,384,128]{2,1,0:T(8,128)(2,1)S(1)}, u32[]{:S(2)}, u32[]{:S(2)}) collective-permute-start(bf16[2,384,128]{2,1,0:T(8,128)(2,1)S(1)} %get-tuple-element.44), channel_id=1, source_target_pairs={{0,1},{1,0},{2,3},{3,2},{4,5},{5,4},{6,7},{7,6},{8,9},{9,8},{10,11... | collective-permute-start | bytes 589832 | tf_op jit(solution)/shard_map/ppermute | solution.py:38
  28.8 1.7 %late_rows.4 = (bf16[8,384,256]{2,1,0:T(8,128)(2,1)S(1)}, bf16[2,384,128]{2,1,0:T(8,128)(2,1)S(1)}, bf16[2,384,128]{2,1,0:T(8,128)(2,1)S(1)}, bf16[2,384,128]{2,1,0:T(8,128)(2,1)S(1)}, bf16[2,384,128]{2,1,0:T(8,128)(2,1)S(1)}) custom-call(s32[8,6]{1,0:T(8,128)S(4)} %get-tuple-element.36.refs_0_, ...), custom_call_target="tpu_custom_call", output_to_operand_aliasing={{0}: (10, {})} | custom-call | bytes 4194304 | tf_op jit(solution)/shard_map/late_rows/pallas_call | solution.py:365
  30.5 0.2 collective-permute-start.12
  30.7 0.7 collective-permute-start.13
  31.4 0.7 collective-permute-start.14
  32.1 1.9 %late_rows.5 = (bf16[8,384,256]{2,1,0:T(8,128)(2,1)S(1)}, bf16[2,384,128]{2,1,0:T(8,128)(2,1)S(1)}, bf16[2,384,128]{2,1,0:T(8,128)(2,1)S(1)}, bf16[2,384,128]{2,1,0:T(8,128)(2,1)S(1)}, bf16[2,384,128]{2,1,0:T(8,128)(2,1)S(1)}) custom-call(s32[8,6]{1,0:T(8,128)S(4)} %get-tuple-element.36.refs_0_, ...), custom_call_target="tpu_custom_call", output_to_operand_aliasing={{0}: (10, {})} | custom-call | bytes 4194304 | tf_op jit(solution)/shard_map/late_rows/pallas_call | solution.py:365
  34.0 7.2 %collective-permute-start.8 = (bf16[2,384,128]{2,1,0:T(8,128)(2,1)S(1)}, bf16[2,384,128]{2,1,0:T(8,128)(2,1)S(1)}, u32[]{:S(2)}, u32[]{:S(2)}) collective-permute-start(bf16[2,384,128]{2,1,0:T(8,128)(2,1)S(1)} %get-tuple-element.52), channel_id=1, source_target_pairs={{0,2},{1,3},{2,0},{3,1},{4,6},{5,7},{6,4},{7,5},{8,10},{9,11},{10,... | collective-permute-start | bytes 589832 | tf_op jit(solution)/shard_map/ppermute | solution.py:38
  41.2 0.3 collective-permute-start.15
  41.5 0.7 collective-permute-start.9
  42.1 0.7 collective-permute-start.10
  42.8 9.8 %collective-permute-start.11 = (bf16[2,384,128]{2,1,0:T(8,128)(2,1)S(1)}, bf16[2,384,128]{2,1,0:T(8,128)(2,1)S(1)}, u32[]{:S(2)}, u32[]{:S(2)}) collective-permute-start(bf16[2,384,128]{2,1,0:T(8,128)(2,1)S(1)} %get-tuple-element.55), channel_id=1, source_target_pairs={{0,1},{1,0},{2,3},{3,2},{4,5},{5,4},{6,7},{7,6},{8,9},{9,8},{10,11... | collective-permute-start | bytes 589832 | tf_op jit(solution)/shard_map/ppermute | solution.py:38
  52.6 2.3 %early_rows.3 = (bf16[8,384,256]{2,1,0:T(8,128)(2,1)S(1)}, f32[8,128,256]{2,1,0:T(8,128)S(1)}, f32[1,1,256]{2,1,0:T(1,128)S(1)}, f32[8,384,256]{2,1,0:T(8,128)S(1)}) custom-call(s32[8,6]{1,0:T(8,128)S(4)} %get-tuple-element.36.refs_0_, s32[1,2,4]{2,1,0:T(2,128)S(4)} %get-tuple-element.37.refs_1_, bf16[8,384,256]{2,1,0:T(8,128)(2,1)S(1)} %get-tuple-element.51.refs_2_, ...), custom_call_target="tpu_custom_call" | custom-call | bytes 4194304 | tf_op jit(solution)/shard_map/early_rows/pallas_call | solution.py:365
  54.9 1.6 %late_rows.6 = (bf16[8,384,256]{2,1,0:T(8,128)(2,1)S(1)}, f32[8,128,256]{2,1,0:T(8,128)S(1)}, f32[1,1,256]{2,1,0:T(1,128)S(1)}) custom-call(s32[8,6]{1,0:T(8,128)S(4)} %get-tuple-element.36.refs_0_, s32[1,2,4]{2,1,0:T(2,128)S(4)} %get-tuple-element.37.refs_1_, ...), custom_call_target="tpu_custom_call", output_to_operand_aliasing={{0}: (10, {}), {1}: (11, {})} | custom-call | bytes 4194304 | tf_op jit(solution)/shard_map/late_rows/pallas_call | solution.py:365
  56.6 2.3 %late_rows.7 = (bf16[8,384,256]{2,1,0:T(8,128)(2,1)S(1)}, f32[8,128,256]{2,1,0:T(8,128)S(1)}, f32[32,1,256]{2,1,0:T(1,128)}) custom-call(s32[8,6]{1,0:T(8,128)S(4)} %get-tuple-element.36.refs_0_, s32[1,2,4]{2,1,0:T(2,128)S(4)} %get-tuple-element.37.refs_1_, ...), custom_call_target="tpu_custom_call", output_to_operand_aliasing={{0}: (10, {}), {1}: (11, {})} | custom-call | bytes 4194304 | tf_op jit(solution)/shard_map/late_rows/pallas_call | solution.py:365
  58.9 9.4 %all-to-all-start = ((f32[32,1,256]{2,1,0:T(1,128)}), f32[32,1,256]{2,1,0:T(1,128)S(1)}, u32[]{:S(2)}, u32[]{:S(2)}) async-start(f32[32,1,256]{2,1,0:T(1,128)} %get-tuple-element.68), calls=%async_computation | async-start | bytes 65536 | tf_op jit(solution)/shard_map/all_to_all | solution.py:452
  68.3 1.1 %copy.24 = bf16[8,384,256]{2,1,0:T(8,128)(2,1)} copy(bf16[8,384,256]{2,1,0:T(8,128)(2,1)S(1)} %get-tuple-element.70) | data formatting | bytes 3145728
  69.4 6.1 %all-to-all-done.sums = f32[32,1,256]{2,1,0:T(1,128)S(1)} async-done(((f32[32,1,256]{2,1,0:T(1,128)}), f32[32,1,256]{2,1,0:T(1,128)S(1)}, u32[]{:S(2)}, u32[]{:S(2)}) %all-to-all-start) | async-done | bytes 32800 | tf_op jit(solution)/shard_map/all_to_all | solution.py:452
  75.5 1.1 %scale.1 = f32[8,128,256]{2,1,0:T(8,128)} custom-call(f32[32,1,256]{2,1,0:T(1,128)S(1)} %all-to-all-done.sums, f32[8,128,256]{2,1,0:T(8,128)S(1)} %get-tuple-element.69.raw), custom_call_target="tpu_custom_call" | custom-call | tf_op jit(solution)/shard_map/scale/pallas_call | solution.py:392
  (27 shorter events, 0.1 us)
Async XLA Ops:
  0.6 12.2 %copy-start = (bf16[8,384,256]{2,1,0:T(8,128)(2,1)S(1)}, bf16[8,384,256]{2,1,0:T(8,128)(2,1)}, u32[]{:S(2)}) copy-start(bf16[8,384,256]{2,1,0:T(8,128)(2,1)} %refs_2_.5) | copy-start | bytes 4718596
  0.6 12.2 %copy-start.3 = (s32[1,4,2]{1,2,0:T(2,128)S(1)}, s32[1,4,2]{1,2,0:T(2,128)}, u32[]{:S(2)}) copy-start(s32[1,4,2]{1,2,0:T(2,128)} %param.13) | copy-start | bytes 100
  0.7 12.2 %copy-start.7 = (f32[256]{0:T(256)S(1)}, f32[256]{0:T(256)}, u32[]{:S(2)}) copy-start(f32[256]{0:T(256)} %param.18) | copy-start | bytes 3076
  0.7 12.2 %copy-start.6 = (s32[256]{0:T(256)S(1)}, s32[256]{0:T(256)}, u32[]{:S(2)}) copy-start(s32[256]{0:T(256)} %param.17) | copy-start | bytes 3076
  0.7 12.2 %copy-start.5 = (s32[256]{0:T(256)S(1)}, s32[256]{0:T(256)}, u32[]{:S(2)}) copy-start(s32[256]{0:T(256)} %param.16) | copy-start | bytes 3076
  0.7 12.2 %copy-start.4 = (s32[256]{0:T(256)S(1)}, s32[256]{0:T(256)}, u32[]{:S(2)}) copy-start(s32[256]{0:T(256)} %param.15) | copy-start | bytes 3076
  0.7 12.2 %copy-start.2 = (s32[8,128]{1,0:T(8,128)S(1)}, s32[8,128]{1,0:T(8,128)}, u32[]{:S(2)}) copy-start(s32[8,128]{1,0:T(8,128)} %refs_4_.1) | copy-start | bytes 12292
  2.8 14.8 %collective-permute-start.4 = (bf16[2,384,128]{2,1,0:T(8,128)(2,1)S(1)}, bf16[2,384,128]{2,1,0:T(8,128)(2,1)S(1)}, u32[]{:S(2)}, u32[]{:S(2)}) collective-permute-start(bf16[2,384,128]{2,1,0:T(8,128)(2,1)S(1)} %get-tuple-element.45), channel_id=1, source_target_pairs={{0,2},{1,3},{2,0},{3,1},{4,6},{5,7},{6,4},{7,5},{8,10},{9,11},{10,... | collective-permute-start | bytes 589832 | tf_op jit(solution)/shard_map/ppermute | solution.py:38
  5.8 12.5 %collective-permute-start.5 = (bf16[2,384,128]{2,1,0:T(8,128)(2,1)S(1)}, bf16[2,384,128]{2,1,0:T(8,128)(2,1)S(1)}, u32[]{:S(2)}, u32[]{:S(2)}) collective-permute-start(bf16[2,384,128]{2,1,0:T(8,128)(2,1)S(1)} %get-tuple-element.46), channel_id=1, source_target_pairs={{2,4},{3,5},{6,8},{7,9},{10,12},{11,13},{14,16},{15,17},{18,20},{1... | collective-permute-start | bytes 589832 | tf_op jit(solution)/shard_map/ppermute | solution.py:38
  6.5 12.5 %collective-permute-start.6 = (bf16[2,384,128]{2,1,0:T(8,128)(2,1)S(1)}, bf16[2,384,128]{2,1,0:T(8,128)(2,1)S(1)}, u32[]{:S(2)}, u32[]{:S(2)}) collective-permute-start(bf16[2,384,128]{2,1,0:T(8,128)(2,1)S(1)} %get-tuple-element.47), channel_id=1, source_target_pairs={{1,2},{3,4},{5,6},{7,8},{9,10},{11,12},{13,14},{15,16},{17,18},{19... | collective-permute-start | bytes 589832 | tf_op jit(solution)/shard_map/ppermute | solution.py:38
  7.2 21.6 %collective-permute-start.7 = (bf16[2,384,128]{2,1,0:T(8,128)(2,1)S(1)}, bf16[2,384,128]{2,1,0:T(8,128)(2,1)S(1)}, u32[]{:S(2)}, u32[]{:S(2)}) collective-permute-start(bf16[2,384,128]{2,1,0:T(8,128)(2,1)S(1)} %get-tuple-element.48), channel_id=1, source_target_pairs={{0,1},{1,0},{2,3},{3,2},{4,5},{5,4},{6,7},{7,6},{8,9},{9,8},{10,11... | collective-permute-start | bytes 589832 | tf_op jit(solution)/shard_map/ppermute | solution.py:38
  12.9 0.7 copy-start.1
  17.6 13.1 %collective-permute-start = (bf16[2,384,128]{2,1,0:T(8,128)(2,1)S(1)}, bf16[2,384,128]{2,1,0:T(8,128)(2,1)S(1)}, u32[]{:S(2)}, u32[]{:S(2)}) collective-permute-start(bf16[2,384,128]{2,1,0:T(8,128)(2,1)S(1)} %get-tuple-element.41), channel_id=1, source_target_pairs={{0,2},{1,3},{2,0},{3,1},{4,6},{5,7},{6,4},{7,5},{8,10},{9,11},{10,... | collective-permute-start | bytes 589832 | tf_op jit(solution)/shard_map/ppermute | solution.py:38
  17.7 13.7 %collective-permute-start.1 = (bf16[2,384,128]{2,1,0:T(8,128)(2,1)S(1)}, bf16[2,384,128]{2,1,0:T(8,128)(2,1)S(1)}, u32[]{:S(2)}, u32[]{:S(2)}) collective-permute-start(bf16[2,384,128]{2,1,0:T(8,128)(2,1)S(1)} %get-tuple-element.42), channel_id=1, source_target_pairs={{2,4},{3,5},{6,8},{7,9},{10,12},{11,13},{14,16},{15,17},{18,20},{1... | collective-permute-start | bytes 589832 | tf_op jit(solution)/shard_map/ppermute | solution.py:38
  18.4 13.7 %collective-permute-start.2 = (bf16[2,384,128]{2,1,0:T(8,128)(2,1)S(1)}, bf16[2,384,128]{2,1,0:T(8,128)(2,1)S(1)}, u32[]{:S(2)}, u32[]{:S(2)}) collective-permute-start(bf16[2,384,128]{2,1,0:T(8,128)(2,1)S(1)} %get-tuple-element.43), channel_id=1, source_target_pairs={{1,2},{3,4},{5,6},{7,8},{9,10},{11,12},{13,14},{15,16},{17,18},{19... | collective-permute-start | bytes 589832 | tf_op jit(solution)/shard_map/ppermute | solution.py:38
  19.0 13.0 %collective-permute-start.3 = (bf16[2,384,128]{2,1,0:T(8,128)(2,1)S(1)}, bf16[2,384,128]{2,1,0:T(8,128)(2,1)S(1)}, u32[]{:S(2)}, u32[]{:S(2)}) collective-permute-start(bf16[2,384,128]{2,1,0:T(8,128)(2,1)S(1)} %get-tuple-element.44), channel_id=1, source_target_pairs={{0,1},{1,0},{2,3},{3,2},{4,5},{5,4},{6,7},{7,6},{8,9},{9,8},{10,11... | collective-permute-start | bytes 589832 | tf_op jit(solution)/shard_map/ppermute | solution.py:38
  30.5 10.9 %collective-permute-start.12 = (bf16[2,384,128]{2,1,0:T(8,128)(2,1)S(1)}, bf16[2,384,128]{2,1,0:T(8,128)(2,1)S(1)}, u32[]{:S(2)}, u32[]{:S(2)}) collective-permute-start(bf16[2,384,128]{2,1,0:T(8,128)(2,1)S(1)} %get-tuple-element.56), channel_id=1, source_target_pairs={{0,2},{1,3},{2,0},{3,1},{4,6},{5,7},{6,4},{7,5},{8,10},{9,11},{10,... | collective-permute-start | bytes 589832 | tf_op jit(solution)/shard_map/ppermute | solution.py:38
  30.7 11.4 %collective-permute-start.13 = (bf16[2,384,128]{2,1,0:T(8,128)(2,1)S(1)}, bf16[2,384,128]{2,1,0:T(8,128)(2,1)S(1)}, u32[]{:S(2)}, u32[]{:S(2)}) collective-permute-start(bf16[2,384,128]{2,1,0:T(8,128)(2,1)S(1)} %get-tuple-element.57), channel_id=1, source_target_pairs={{2,4},{3,5},{6,8},{7,9},{10,12},{11,13},{14,16},{15,17},{18,20},{1... | collective-permute-start | bytes 589832 | tf_op jit(solution)/shard_map/ppermute | solution.py:38
  31.4 11.5 %collective-permute-start.14 = (bf16[2,384,128]{2,1,0:T(8,128)(2,1)S(1)}, bf16[2,384,128]{2,1,0:T(8,128)(2,1)S(1)}, u32[]{:S(2)}, u32[]{:S(2)}) collective-permute-start(bf16[2,384,128]{2,1,0:T(8,128)(2,1)S(1)} %get-tuple-element.58), channel_id=1, source_target_pairs={{1,2},{3,4},{5,6},{7,8},{9,10},{11,12},{13,14},{15,16},{17,18},{19... | collective-permute-start | bytes 589832 | tf_op jit(solution)/shard_map/ppermute | solution.py:38
  34.0 22.6 %collective-permute-start.8 = (bf16[2,384,128]{2,1,0:T(8,128)(2,1)S(1)}, bf16[2,384,128]{2,1,0:T(8,128)(2,1)S(1)}, u32[]{:S(2)}, u32[]{:S(2)}) collective-permute-start(bf16[2,384,128]{2,1,0:T(8,128)(2,1)S(1)} %get-tuple-element.52), channel_id=1, source_target_pairs={{0,2},{1,3},{2,0},{3,1},{4,6},{5,7},{6,4},{7,5},{8,10},{9,11},{10,... | collective-permute-start | bytes 589832 | tf_op jit(solution)/shard_map/ppermute | solution.py:38
  41.2 13.7 %collective-permute-start.15 = (bf16[2,384,128]{2,1,0:T(8,128)(2,1)S(1)}, bf16[2,384,128]{2,1,0:T(8,128)(2,1)S(1)}, u32[]{:S(2)}, u32[]{:S(2)}) collective-permute-start(bf16[2,384,128]{2,1,0:T(8,128)(2,1)S(1)} %get-tuple-element.59), channel_id=1, source_target_pairs={{0,1},{1,0},{2,3},{3,2},{4,5},{5,4},{6,7},{7,6},{8,9},{9,8},{10,11... | collective-permute-start | bytes 589832 | tf_op jit(solution)/shard_map/ppermute | solution.py:38
  41.5 15.1 %collective-permute-start.9 = (bf16[2,384,128]{2,1,0:T(8,128)(2,1)S(1)}, bf16[2,384,128]{2,1,0:T(8,128)(2,1)S(1)}, u32[]{:S(2)}, u32[]{:S(2)}) collective-permute-start(bf16[2,384,128]{2,1,0:T(8,128)(2,1)S(1)} %get-tuple-element.53), channel_id=1, source_target_pairs={{2,4},{3,5},{6,8},{7,9},{10,12},{11,13},{14,16},{15,17},{18,20},{1... | collective-permute-start | bytes 589832 | tf_op jit(solution)/shard_map/ppermute | solution.py:38
  42.1 14.4 %collective-permute-start.10 = (bf16[2,384,128]{2,1,0:T(8,128)(2,1)S(1)}, bf16[2,384,128]{2,1,0:T(8,128)(2,1)S(1)}, u32[]{:S(2)}, u32[]{:S(2)}) collective-permute-start(bf16[2,384,128]{2,1,0:T(8,128)(2,1)S(1)} %get-tuple-element.54), channel_id=1, source_target_pairs={{1,2},{3,4},{5,6},{7,8},{9,10},{11,12},{13,14},{15,16},{17,18},{19... | collective-permute-start | bytes 589832 | tf_op jit(solution)/shard_map/ppermute | solution.py:38
  42.8 13.8 %collective-permute-start.11 = (bf16[2,384,128]{2,1,0:T(8,128)(2,1)S(1)}, bf16[2,384,128]{2,1,0:T(8,128)(2,1)S(1)}, u32[]{:S(2)}, u32[]{:S(2)}) collective-permute-start(bf16[2,384,128]{2,1,0:T(8,128)(2,1)S(1)} %get-tuple-element.55), channel_id=1, source_target_pairs={{0,1},{1,0},{2,3},{3,2},{4,5},{5,4},{6,7},{7,6},{8,9},{9,8},{10,11... | collective-permute-start | bytes 589832 | tf_op jit(solution)/shard_map/ppermute | solution.py:38
  58.9 16.6 %all-to-all-start = ((f32[32,1,256]{2,1,0:T(1,128)}), f32[32,1,256]{2,1,0:T(1,128)S(1)}, u32[]{:S(2)}, u32[]{:S(2)}) async-start(f32[32,1,256]{2,1,0:T(1,128)} %get-tuple-element.68), calls=%async_computation | async-start | bytes 65536 | tf_op jit(solution)/shard_map/all_to_all | solution.py:452

commit v2 on v1

--- a/solution.py
+++ b/solution.py
@@ -419,7 +419,7 @@
     steps = snapshots.shape[0]
     devices = lax.axis_size("dom")
     halo = jnp.swapaxes(halo_send, 1, 2)
-    facts = [wet_cells, snapshots] + [
+    facts = [wet_cells, in_hbm(snapshots)] + [
         v[None] for v in (gauge_cells, window_first, window_len, gauge_gain)
     ]
     width = adjoint_end.shape[2]

time: 76.6 us -> 75.6 us (0.987)
    unnamed x17 -> x15, local copies, waits for them, and re-layouts: 1.91 us -> 1.17 us
  transfers between devices with their start and end apart: 17 -> 17, of which waited for: 1 -> 1; matrix products, arithmetic and copies ran while one was open for 1% -> 2% of each run, Pallas kernels for 15% -> 15%
where the time goes in v2:
time: 75.6 us; the launch traced here: 75.8 us
  starting transfers between devices  50.1 us (66%)
  Pallas kernels  17.2 us (23%)
  waiting for transfers between devices  6.15 us (8%)
  local copies, waits for them, and re-layouts  1.17 us (2%)
  between operations  1.1 us (1%)
    ppermute x16, starting transfers between devices, exchange(): return {r: lax.ppermute(sends[r], 'dom', pairs[r]) for r in ROUTES}  41.3 us
    pallas_call x6, Pallas kernels, step_rows(): pl.pallas_call(functools.partial(step_kernel, late, last, step, part, fin...  13.9 us
    all_to_all x1, starting transfers between devices, per_device(): sums = lax.all_to_all(squares, 'dom', 0, 0, tiled=True)  8.77 us
    all_to_all x1, waiting for transfers between devices, per_device(): sums = lax.all_to_all(squares, 'dom', 0, 0, tiled=True)  6.1 us
    pallas_call x1, Pallas kernels, pick_sends(): pl.pallas_call(functools.partial(pick_kernel, part), name='pick_sends', o...  2.2 us
  transfers between devices with their start and end apart: 17, of which 1 were waited for; matrix products, arithmetic and copies ran while one was open for 2% of the time, Pallas kernels for 15%

profile of v2, /device:TPU:0, one launch (start us, length us, event | category | flops | bytes accessed | tf_op | source)
XLA Modules:
  0.0 75.8 jit_solution(4092225723224958565)
XLA Ops:
  0.7 2.2 %pick_sends.1 = (bf16[2,384,128]{2,1,0:T(8,128)(2,1)S(1)}, bf16[2,384,128]{2,1,0:T(8,128)(2,1)S(1)}, bf16[2,384,128]{2,1,0:T(8,128)(2,1)S(1)}, bf16[2,384,128]{2,1,0:T(8,128)(2,1)S(1)}) custom-call(s32[1,2,4]{2,1,0:T(2,128)} %bitcast.5, bf16[8,384,256]{2,1,0:T(8,128)(2,1)} %refs_2_.5), custom_call_target="tpu_custom_call" | custom-call | bytes 4194304 | tf_op jit(solution)/shard_map/pick_sends/pallas_call | solution.py:67
  2.9 2.9 %collective-permute-start.4 = (bf16[2,384,128]{2,1,0:T(8,128)(2,1)S(1)}, bf16[2,384,128]{2,1,0:T(8,128)(2,1)S(1)}, u32[]{:S(2)}, u32[]{:S(2)}) collective-permute-start(bf16[2,384,128]{2,1,0:T(8,128)(2,1)S(1)} %get-tuple-element.45), channel_id=1, source_target_pairs={{0,2},{1,3},{2,0},{3,1},{4,6},{5,7},{6,4},{7,5},{8,10},{9,11},{10,... | collective-permute-start | bytes 589832 | tf_op jit(solution)/shard_map/ppermute | solution.py:38
  5.8 0.7 collective-permute-start.5
  6.5 0.7 collective-permute-start.6
  7.2 5.6 %collective-permute-start.7 = (bf16[2,384,128]{2,1,0:T(8,128)(2,1)S(1)}, bf16[2,384,128]{2,1,0:T(8,128)(2,1)S(1)}, u32[]{:S(2)}, u32[]{:S(2)}) collective-permute-start(bf16[2,384,128]{2,1,0:T(8,128)(2,1)S(1)} %get-tuple-element.48), channel_id=1, source_target_pairs={{0,1},{1,0},{2,3},{3,2},{4,5},{5,4},{6,7},{7,6},{8,9},{9,8},{10,11... | collective-permute-start | bytes 589832 | tf_op jit(solution)/shard_map/ppermute | solution.py:38
  12.9 4.1 %early_rows.2 = (bf16[8,384,256]{2,1,0:T(8,128)(2,1)S(1)}, f32[8,128,8]{2,1,0:T(8,128)S(1)}, f32[4,256]{1,0:T(4,128)S(1)}, bf16[8,6,384,384]{3,2,1,0:T(8,128)(2,...) custom-call(s32[8,6]{1,0:T(8,128)} %refs_0_.1, ...), custom_call_target="tpu_custom_call" | custom-call | bytes 4194304 | tf_op jit(solution)/shard_map/early_rows/pallas_call | solution.py:365
  17.0 0.1 collective-permute-start
  17.1 0.0 collective-permute-done.4.refs_6_
  17.1 0.7 collective-permute-start.1
  17.8 0.0 collective-permute-done.5.refs_7_
  17.8 0.7 collective-permute-start.2
  18.5 0.0 collective-permute-done.6.refs_8_
  18.5 6.7 %collective-permute-start.3 = (bf16[2,384,128]{2,1,0:T(8,128)(2,1)S(1)}, bf16[2,384,128]{2,1,0:T(8,128)(2,1)S(1)}, u32[]{:S(2)}, u32[]{:S(2)}) collective-permute-start(bf16[2,384,128]{2,1,0:T(8,128)(2,1)S(1)} %get-tuple-element.44), channel_id=1, source_target_pairs={{0,1},{1,0},{2,3},{3,2},{4,5},{5,4},{6,7},{7,6},{8,9},{9,8},{10,11... | collective-permute-start | bytes 589832 | tf_op jit(solution)/shard_map/ppermute | solution.py:38
  25.2 0.0 collective-permute-done.7.refs_9_
  25.2 1.7 %late_rows.4 = (bf16[8,384,256]{2,1,0:T(8,128)(2,1)S(1)}, bf16[2,384,128]{2,1,0:T(8,128)(2,1)S(1)}, bf16[2,384,128]{2,1,0:T(8,128)(2,1)S(1)}, bf16[2,384,128]{2,1,0:T(8,128)(2,1)S(1)}, bf16[2,384,128]{2,1,0:T(8,128)(2,1)S(1)}) custom-call(s32[8,6]{1,0:T(8,128)S(4)} %get-tuple-element.36.refs_0_, ...), custom_call_target="tpu_custom_call", output_to_operand_aliasing={{0}: (10, {})} | custom-call | bytes 4194304 | tf_op jit(solution)/shard_map/late_rows/pallas_call | solution.py:365
  26.9 1.1 %collective-permute-start.12 = (bf16[2,384,128]{2,1,0:T(8,128)(2,1)S(1)}, bf16[2,384,128]{2,1,0:T(8,128)(2,1)S(1)}, u32[]{:S(2)}, u32[]{:S(2)}) collective-permute-start(bf16[2,384,128]{2,1,0:T(8,128)(2,1)S(1)} %get-tuple-element.56), channel_id=1, source_target_pairs={{0,2},{1,3},{2,0},{3,1},{4,6},{5,7},{6,4},{7,5},{8,10},{9,11},{10,... | collective-permute-start | bytes 589832 | tf_op jit(solution)/shard_map/ppermute | solution.py:38
  27.9 0.7 collective-permute-start.13
  28.6 0.7 collective-permute-start.14
  29.3 0.0 collective-permute-done.2.refs_8_
  29.3 1.9 %late_rows.5 = (bf16[8,384,256]{2,1,0:T(8,128)(2,1)S(1)}, bf16[2,384,128]{2,1,0:T(8,128)(2,1)S(1)}, bf16[2,384,128]{2,1,0:T(8,128)(2,1)S(1)}, bf16[2,384,128]{2,1,0:T(8,128)(2,1)S(1)}, bf16[2,384,128]{2,1,0:T(8,128)(2,1)S(1)}) custom-call(s32[8,6]{1,0:T(8,128)S(4)} %get-tuple-element.36.refs_0_, ...), custom_call_target="tpu_custom_call", output_to_operand_aliasing={{0}: (10, {})} | custom-call | bytes 4194304 | tf_op jit(solution)/shard_map/late_rows/pallas_call | solution.py:365
  31.2 6.4 %collective-permute-start.8 = (bf16[2,384,128]{2,1,0:T(8,128)(2,1)S(1)}, bf16[2,384,128]{2,1,0:T(8,128)(2,1)S(1)}, u32[]{:S(2)}, u32[]{:S(2)}) collective-permute-start(bf16[2,384,128]{2,1,0:T(8,128)(2,1)S(1)} %get-tuple-element.52), channel_id=1, source_target_pairs={{0,2},{1,3},{2,0},{3,1},{4,6},{5,7},{6,4},{7,5},{8,10},{9,11},{10,... | collective-permute-start | bytes 589832 | tf_op jit(solution)/shard_map/ppermute | solution.py:38
  37.7 0.3 collective-permute-start.15
  38.0 0.7 collective-permute-start.9
  38.6 0.7 collective-permute-start.10
  39.3 12.9 %collective-permute-start.11 = (bf16[2,384,128]{2,1,0:T(8,128)(2,1)S(1)}, bf16[2,384,128]{2,1,0:T(8,128)(2,1)S(1)}, u32[]{:S(2)}, u32[]{:S(2)}) collective-permute-start(bf16[2,384,128]{2,1,0:T(8,128)(2,1)S(1)} %get-tuple-element.55), channel_id=1, source_target_pairs={{0,1},{1,0},{2,3},{3,2},{4,5},{5,4},{6,7},{7,6},{8,9},{9,8},{10,11... | collective-permute-start | bytes 589832 | tf_op jit(solution)/shard_map/ppermute | solution.py:38
  52.2 2.3 %early_rows.3 = (bf16[8,384,256]{2,1,0:T(8,128)(2,1)S(1)}, f32[8,128,256]{2,1,0:T(8,128)S(1)}, f32[1,1,256]{2,1,0:T(1,128)S(1)}, f32[8,384,256]{2,1,0:T(8,128)S(1)}) custom-call(s32[8,6]{1,0:T(8,128)S(4)} %get-tuple-element.36.refs_0_, s32[1,2,4]{2,1,0:T(2,128)S(4)} %get-tuple-element.37.refs_1_, bf16[8,384,256]{2,1,0:T(8,128)(2,1)S(1)} %get-tuple-element.51.refs_2_, ...), custom_call_target="tpu_custom_call" | custom-call | bytes 4194304 | tf_op jit(solution)/shard_map/early_rows/pallas_call | solution.py:365
  54.5 1.6 %late_rows.6 = (bf16[8,384,256]{2,1,0:T(8,128)(2,1)S(1)}, f32[8,128,256]{2,1,0:T(8,128)S(1)}, f32[1,1,256]{2,1,0:T(1,128)S(1)}) custom-call(s32[8,6]{1,0:T(8,128)S(4)} %get-tuple-element.36.refs_0_, s32[1,2,4]{2,1,0:T(2,128)S(4)} %get-tuple-element.37.refs_1_, ...), custom_call_target="tpu_custom_call", output_to_operand_aliasing={{0}: (10, {}), {1}: (11, {})} | custom-call | bytes 4194304 | tf_op jit(solution)/shard_map/late_rows/pallas_call | solution.py:365
  56.2 2.3 %late_rows.7 = (bf16[8,384,256]{2,1,0:T(8,128)(2,1)S(1)}, f32[8,128,256]{2,1,0:T(8,128)S(1)}, f32[32,1,256]{2,1,0:T(1,128)}) custom-call(s32[8,6]{1,0:T(8,128)S(4)} %get-tuple-element.36.refs_0_, s32[1,2,4]{2,1,0:T(2,128)S(4)} %get-tuple-element.37.refs_1_, ...), custom_call_target="tpu_custom_call", output_to_operand_aliasing={{0}: (10, {}), {1}: (11, {})} | custom-call | bytes 4194304 | tf_op jit(solution)/shard_map/late_rows/pallas_call | solution.py:365
  58.5 8.8 %all-to-all-start = ((f32[32,1,256]{2,1,0:T(1,128)}), f32[32,1,256]{2,1,0:T(1,128)S(1)}, u32[]{:S(2)}, u32[]{:S(2)}) async-start(f32[32,1,256]{2,1,0:T(1,128)} %get-tuple-element.68), calls=%async_computation | async-start | bytes 65536 | tf_op jit(solution)/shard_map/all_to_all | solution.py:452
  67.3 1.1 %copy.24 = bf16[8,384,256]{2,1,0:T(8,128)(2,1)} copy(bf16[8,384,256]{2,1,0:T(8,128)(2,1)S(1)} %get-tuple-element.70) | data formatting | bytes 3145728
  68.4 6.1 %all-to-all-done.sums = f32[32,1,256]{2,1,0:T(1,128)S(1)} async-done(((f32[32,1,256]{2,1,0:T(1,128)}), f32[32,1,256]{2,1,0:T(1,128)S(1)}, u32[]{:S(2)}, u32[]{:S(2)}) %all-to-all-start) | async-done | bytes 32800 | tf_op jit(solution)/shard_map/all_to_all | solution.py:452
  74.5 1.1 %scale.1 = f32[8,128,256]{2,1,0:T(8,128)} custom-call(f32[32,1,256]{2,1,0:T(1,128)S(1)} %all-to-all-done.sums, f32[8,128,256]{2,1,0:T(8,128)S(1)} %get-tuple-element.69.raw), custom_call_target="tpu_custom_call" | custom-call | tf_op jit(solution)/shard_map/scale/pallas_call | solution.py:392
  (25 shorter events, 0.1 us)
Async XLA Ops:
  0.6 12.2 %copy-start = (bf16[8,384,256]{2,1,0:T(8,128)(2,1)S(1)}, bf16[8,384,256]{2,1,0:T(8,128)(2,1)}, u32[]{:S(2)}) copy-start(bf16[8,384,256]{2,1,0:T(8,128)(2,1)} %refs_2_.5) | copy-start | bytes 4718596
  0.6 12.2 %copy-start.2 = (s32[1,4,2]{1,2,0:T(2,128)S(1)}, s32[1,4,2]{1,2,0:T(2,128)}, u32[]{:S(2)}) copy-start(s32[1,4,2]{1,2,0:T(2,128)} %param.13) | copy-start | bytes 100
  0.7 12.2 %copy-start.6 = (f32[256]{0:T(256)S(1)}, f32[256]{0:T(256)}, u32[]{:S(2)}) copy-start(f32[256]{0:T(256)} %param.18) | copy-start | bytes 3076
  0.7 12.2 %copy-start.5 = (s32[256]{0:T(256)S(1)}, s32[256]{0:T(256)}, u32[]{:S(2)}) copy-start(s32[256]{0:T(256)} %param.17) | copy-start | bytes 3076
  0.7 12.2 %copy-start.4 = (s32[256]{0:T(256)S(1)}, s32[256]{0:T(256)}, u32[]{:S(2)}) copy-start(s32[256]{0:T(256)} %param.16) | copy-start | bytes 3076
  0.7 12.2 %copy-start.3 = (s32[256]{0:T(256)S(1)}, s32[256]{0:T(256)}, u32[]{:S(2)}) copy-start(s32[256]{0:T(256)} %param.15) | copy-start | bytes 3076
  0.7 12.2 %copy-start.1 = (s32[8,128]{1,0:T(8,128)S(1)}, s32[8,128]{1,0:T(8,128)}, u32[]{:S(2)}) copy-start(s32[8,128]{1,0:T(8,128)} %refs_4_.1) | copy-start | bytes 12292
  2.9 14.2 %collective-permute-start.4 = (bf16[2,384,128]{2,1,0:T(8,128)(2,1)S(1)}, bf16[2,384,128]{2,1,0:T(8,128)(2,1)S(1)}, u32[]{:S(2)}, u32[]{:S(2)}) collective-permute-start(bf16[2,384,128]{2,1,0:T(8,128)(2,1)S(1)} %get-tuple-element.45), channel_id=1, source_target_pairs={{0,2},{1,3},{2,0},{3,1},{4,6},{5,7},{6,4},{7,5},{8,10},{9,11},{10,... | collective-permute-start | bytes 589832 | tf_op jit(solution)/shard_map/ppermute | solution.py:38
  5.8 11.9 %collective-permute-start.5 = (bf16[2,384,128]{2,1,0:T(8,128)(2,1)S(1)}, bf16[2,384,128]{2,1,0:T(8,128)(2,1)S(1)}, u32[]{:S(2)}, u32[]{:S(2)}) collective-permute-start(bf16[2,384,128]{2,1,0:T(8,128)(2,1)S(1)} %get-tuple-element.46), channel_id=1, source_target_pairs={{2,4},{3,5},{6,8},{7,9},{10,12},{11,13},{14,16},{15,17},{18,20},{1... | collective-permute-start | bytes 589832 | tf_op jit(solution)/shard_map/ppermute | solution.py:38
  6.5 12.0 %collective-permute-start.6 = (bf16[2,384,128]{2,1,0:T(8,128)(2,1)S(1)}, bf16[2,384,128]{2,1,0:T(8,128)(2,1)S(1)}, u32[]{:S(2)}, u32[]{:S(2)}) collective-permute-start(bf16[2,384,128]{2,1,0:T(8,128)(2,1)S(1)} %get-tuple-element.47), channel_id=1, source_target_pairs={{1,2},{3,4},{5,6},{7,8},{9,10},{11,12},{13,14},{15,16},{17,18},{19... | collective-permute-start | bytes 589832 | tf_op jit(solution)/shard_map/ppermute | solution.py:38
  7.2 18.0 %collective-permute-start.7 = (bf16[2,384,128]{2,1,0:T(8,128)(2,1)S(1)}, bf16[2,384,128]{2,1,0:T(8,128)(2,1)S(1)}, u32[]{:S(2)}, u32[]{:S(2)}) collective-permute-start(bf16[2,384,128]{2,1,0:T(8,128)(2,1)S(1)} %get-tuple-element.48), channel_id=1, source_target_pairs={{0,1},{1,0},{2,3},{3,2},{4,5},{5,4},{6,7},{7,6},{8,9},{9,8},{10,11... | collective-permute-start | bytes 589832 | tf_op jit(solution)/shard_map/ppermute | solution.py:38
  17.0 10.9 %collective-permute-start = (bf16[2,384,128]{2,1,0:T(8,128)(2,1)S(1)}, bf16[2,384,128]{2,1,0:T(8,128)(2,1)S(1)}, u32[]{:S(2)}, u32[]{:S(2)}) collective-permute-start(bf16[2,384,128]{2,1,0:T(8,128)(2,1)S(1)} %get-tuple-element.41), channel_id=1, source_target_pairs={{0,2},{1,3},{2,0},{3,1},{4,6},{5,7},{6,4},{7,5},{8,10},{9,11},{10,... | collective-permute-start | bytes 589832 | tf_op jit(solution)/shard_map/ppermute | solution.py:38
  17.1 11.5 %collective-permute-start.1 = (bf16[2,384,128]{2,1,0:T(8,128)(2,1)S(1)}, bf16[2,384,128]{2,1,0:T(8,128)(2,1)S(1)}, u32[]{:S(2)}, u32[]{:S(2)}) collective-permute-start(bf16[2,384,128]{2,1,0:T(8,128)(2,1)S(1)} %get-tuple-element.42), channel_id=1, source_target_pairs={{2,4},{3,5},{6,8},{7,9},{10,12},{11,13},{14,16},{15,17},{18,20},{1... | collective-permute-start | bytes 589832 | tf_op jit(solution)/shard_map/ppermute | solution.py:38
  17.8 11.5 %collective-permute-start.2 = (bf16[2,384,128]{2,1,0:T(8,128)(2,1)S(1)}, bf16[2,384,128]{2,1,0:T(8,128)(2,1)S(1)}, u32[]{:S(2)}, u32[]{:S(2)}) collective-permute-start(bf16[2,384,128]{2,1,0:T(8,128)(2,1)S(1)} %get-tuple-element.43), channel_id=1, source_target_pairs={{1,2},{3,4},{5,6},{7,8},{9,10},{11,12},{13,14},{15,16},{17,18},{19... | collective-permute-start | bytes 589832 | tf_op jit(solution)/shard_map/ppermute | solution.py:38
  18.5 10.8 %collective-permute-start.3 = (bf16[2,384,128]{2,1,0:T(8,128)(2,1)S(1)}, bf16[2,384,128]{2,1,0:T(8,128)(2,1)S(1)}, u32[]{:S(2)}, u32[]{:S(2)}) collective-permute-start(bf16[2,384,128]{2,1,0:T(8,128)(2,1)S(1)} %get-tuple-element.44), channel_id=1, source_target_pairs={{0,1},{1,0},{2,3},{3,2},{4,5},{5,4},{6,7},{7,6},{8,9},{9,8},{10,11... | collective-permute-start | bytes 589832 | tf_op jit(solution)/shard_map/ppermute | solution.py:38
  26.9 11.1 %collective-permute-start.12 = (bf16[2,384,128]{2,1,0:T(8,128)(2,1)S(1)}, bf16[2,384,128]{2,1,0:T(8,128)(2,1)S(1)}, u32[]{:S(2)}, u32[]{:S(2)}) collective-permute-start(bf16[2,384,128]{2,1,0:T(8,128)(2,1)S(1)} %get-tuple-element.56), channel_id=1, source_target_pairs={{0,2},{1,3},{2,0},{3,1},{4,6},{5,7},{6,4},{7,5},{8,10},{9,11},{10,... | collective-permute-start | bytes 589832 | tf_op jit(solution)/shard_map/ppermute | solution.py:38
  27.9 10.7 %collective-permute-start.13 = (bf16[2,384,128]{2,1,0:T(8,128)(2,1)S(1)}, bf16[2,384,128]{2,1,0:T(8,128)(2,1)S(1)}, u32[]{:S(2)}, u32[]{:S(2)}) collective-permute-start(bf16[2,384,128]{2,1,0:T(8,128)(2,1)S(1)} %get-tuple-element.57), channel_id=1, source_target_pairs={{2,4},{3,5},{6,8},{7,9},{10,12},{11,13},{14,16},{15,17},{18,20},{1... | collective-permute-start | bytes 589832 | tf_op jit(solution)/shard_map/ppermute | solution.py:38
  28.6 10.7 %collective-permute-start.14 = (bf16[2,384,128]{2,1,0:T(8,128)(2,1)S(1)}, bf16[2,384,128]{2,1,0:T(8,128)(2,1)S(1)}, u32[]{:S(2)}, u32[]{:S(2)}) collective-permute-start(bf16[2,384,128]{2,1,0:T(8,128)(2,1)S(1)} %get-tuple-element.58), channel_id=1, source_target_pairs={{1,2},{3,4},{5,6},{7,8},{9,10},{11,12},{13,14},{15,16},{17,18},{19... | collective-permute-start | bytes 589832 | tf_op jit(solution)/shard_map/ppermute | solution.py:38
  31.2 24.9 %collective-permute-start.8 = (bf16[2,384,128]{2,1,0:T(8,128)(2,1)S(1)}, bf16[2,384,128]{2,1,0:T(8,128)(2,1)S(1)}, u32[]{:S(2)}, u32[]{:S(2)}) collective-permute-start(bf16[2,384,128]{2,1,0:T(8,128)(2,1)S(1)} %get-tuple-element.52), channel_id=1, source_target_pairs={{0,2},{1,3},{2,0},{3,1},{4,6},{5,7},{6,4},{7,5},{8,10},{9,11},{10,... | collective-permute-start | bytes 589832 | tf_op jit(solution)/shard_map/ppermute | solution.py:38
  37.7 16.9 %collective-permute-start.15 = (bf16[2,384,128]{2,1,0:T(8,128)(2,1)S(1)}, bf16[2,384,128]{2,1,0:T(8,128)(2,1)S(1)}, u32[]{:S(2)}, u32[]{:S(2)}) collective-permute-start(bf16[2,384,128]{2,1,0:T(8,128)(2,1)S(1)} %get-tuple-element.59), channel_id=1, source_target_pairs={{0,1},{1,0},{2,3},{3,2},{4,5},{5,4},{6,7},{7,6},{8,9},{9,8},{10,11... | collective-permute-start | bytes 589832 | tf_op jit(solution)/shard_map/ppermute | solution.py:38
  38.0 18.2 %collective-permute-start.9 = (bf16[2,384,128]{2,1,0:T(8,128)(2,1)S(1)}, bf16[2,384,128]{2,1,0:T(8,128)(2,1)S(1)}, u32[]{:S(2)}, u32[]{:S(2)}) collective-permute-start(bf16[2,384,128]{2,1,0:T(8,128)(2,1)S(1)} %get-tuple-element.53), channel_id=1, source_target_pairs={{2,4},{3,5},{6,8},{7,9},{10,12},{11,13},{14,16},{15,17},{18,20},{1... | collective-permute-start | bytes 589832 | tf_op jit(solution)/shard_map/ppermute | solution.py:38
  38.6 17.6 %collective-permute-start.10 = (bf16[2,384,128]{2,1,0:T(8,128)(2,1)S(1)}, bf16[2,384,128]{2,1,0:T(8,128)(2,1)S(1)}, u32[]{:S(2)}, u32[]{:S(2)}) collective-permute-start(bf16[2,384,128]{2,1,0:T(8,128)(2,1)S(1)} %get-tuple-element.54), channel_id=1, source_target_pairs={{1,2},{3,4},{5,6},{7,8},{9,10},{11,12},{13,14},{15,16},{17,18},{19... | collective-permute-start | bytes 589832 | tf_op jit(solution)/shard_map/ppermute | solution.py:38
  39.3 16.9 %collective-permute-start.11 = (bf16[2,384,128]{2,1,0:T(8,128)(2,1)S(1)}, bf16[2,384,128]{2,1,0:T(8,128)(2,1)S(1)}, u32[]{:S(2)}, u32[]{:S(2)}) collective-permute-start(bf16[2,384,128]{2,1,0:T(8,128)(2,1)S(1)} %get-tuple-element.55), channel_id=1, source_target_pairs={{0,1},{1,0},{2,3},{3,2},{4,5},{5,4},{6,7},{7,6},{8,9},{9,8},{10,11... | collective-permute-start | bytes 589832 | tf_op jit(solution)/shard_map/ppermute | solution.py:38
  58.5 16.0 %all-to-all-start = ((f32[32,1,256]{2,1,0:T(1,128)}), f32[32,1,256]{2,1,0:T(1,128)S(1)}, u32[]{:S(2)}, u32[]{:S(2)}) async-start(f32[32,1,256]{2,1,0:T(1,128)} %get-tuple-element.68), calls=%async_computation | async-start | bytes 65536 | tf_op jit(solution)/shard_map/all_to_all | solution.py:452
